TPU v7x, 32 devices: a whole 2x2x4 slice. The times are simulated.
32 devices in a mesh: view: 8 (over y, x, core), strip: 4 (over z).
Axes of the slice: x: 2, y: 2, z: 4, core: 2. Of those that a mesh axis runs over, the one named last changes fastest.
Arguments:
- tokens: bfloat16 [8, 512, 1536], P('view', 'strip'), may hold values from -48 to 48
- source_ids: int32 [8, 4, 5], replicated, may hold values from 0 to 31, as said below
- source_count: int32 [8, 4], replicated, may hold values from 2 to 5, as said below
- self_query: bfloat16 [1536, 1536], P(None, 'strip'), may hold values from -24 to 24
- self_key: bfloat16 [1536, 1536], P(None, 'strip'), may hold values from -24 to 24
- self_value: bfloat16 [1536, 1536], P(None, 'strip'), may hold values from -0.15625 to 0.15625
- self_out: bfloat16 [1536, 1536], P('strip'), may hold values from -1.1953125 to 1.1953125
- cross_query: bfloat16 [1536, 1536], P(None, 'strip'), may hold values from -24 to 24
- cross_key: bfloat16 [1536, 1536], P(None, 'strip'), may hold values from -24 to 24
- cross_value: bfloat16 [1536, 1536], P(None, 'strip'), may hold values from -0.15625 to 0.15625
- cross_out: bfloat16 [1536, 1536], P('strip'), may hold values from -1.1953125 to 1.1953125
- mlp_up: bfloat16 [1536, 6144], P(None, 'strip'), may hold values from -0.15625 to 0.15625
- mlp_down: bfloat16 [6144, 1536], P('strip'), may hold values from -0.078125 to 0.078125
Outputs:
- mixed: bfloat16 [8, 512, 1536], P('view', 'strip')
Inputs may be any that keep to these rules, and one draw needn't show every extreme that they name: `source_ids`: entry k of strip s of view v names a strip of another view than v; entries with k >= source_count[v, s] are unused. Among all 20 entries of one destination view, used or not, each other view is named at most 3 times, and some view exactly 3 times. `source_count`: every view has a strip with all 5 entries in use.
All inputs are finite; a program needn't handle non-finite values.
Results may differ from a plain program's by a relative error of at most 0.015.
Values may be sent and summed in bfloat16 or wider, within the bound.
A program may use at most 128 MiB of HBM per device.

v0:
```python
import math

import jax
import jax.numpy as jnp
from jax import lax
from jax.sharding import PartitionSpec as P

HEAD_DIM = 64
SLOTS = 5


def rms_rows(values_in):
    widened = values_in.astype(jnp.float32)
    scaled = widened * lax.rsqrt(jnp.mean(widened * widened, axis=-1, keepdims=True) + 1e-06)
    return scaled.astype(jnp.bfloat16)


def attend_heads(query_heads, key_heads, value_heads, key_mask):
    scale = 1.0 / math.sqrt(HEAD_DIM)
    scores = (
        jnp.einsum("qhe,khe->hqk", query_heads, key_heads, preferred_element_type=jnp.float32)
        * scale
    )
    scores = jnp.where(key_mask[None, None, :], scores, -1e30)
    weights = jax.nn.softmax(scores, axis=-1).astype(jnp.bfloat16)
    mixed_heads = jnp.einsum(
        "hqk,khe->qhe", weights, value_heads, preferred_element_type=jnp.float32
    )
    return mixed_heads.reshape(mixed_heads.shape[0], -1).astype(jnp.bfloat16)


def branch_term(mixed_rows, weight):
    return jnp.dot(mixed_rows, weight, preferred_element_type=jnp.float32)


def per_device(
    tokens,
    source_ids,
    source_count,
    self_query,
    self_key,
    self_value,
    self_out,
    cross_query,
    cross_key,
    cross_value,
    cross_out,
    mlp_up,
    mlp_down,
):
    n_view = lax.axis_size("view")
    n_strip = lax.axis_size("strip")
    my_view = lax.axis_index("view")
    strip_rows = tokens.shape[1]
    head_cols = self_query.shape[1]
    heads_here = head_cols // HEAD_DIM
    capacity = (n_strip * SLOTS + n_view - 2) // (n_view - 1)
    normed = rms_rows(tokens[0])
    stacked = jnp.concatenate(
        [self_query, self_key, self_value, cross_query, cross_key, cross_value, mlp_up], 1
    )
    split_at = 6 * head_cols
    product = jnp.dot(
        lax.all_gather(normed, "strip", axis=0, tiled=True),
        stacked,
        preferred_element_type=jnp.float32,
    )
    projected = jnp.concatenate(
        [product[:, :split_at], jax.nn.gelu(product[:, split_at:])], 1
    ).astype(jnp.bfloat16)
    total_rows = projected.shape[0]
    flat_ids = source_ids.reshape(n_view, -1)
    source_view = flat_ids // n_strip
    source_strip = flat_ids % n_strip
    entry_count = flat_ids.shape[1]
    entry_order = jnp.arange(entry_count, dtype=jnp.int32)
    earlier = entry_order[None, :] < entry_order[:, None]
    same_view = source_view[:, :, None] == source_view[:, None, :]
    slot_rank = jnp.sum(jnp.logical_and(same_view, earlier[None]), axis=2)
    slot_index = jnp.arange(capacity, dtype=jnp.int32)
    slot_match = jnp.logical_and(
        (source_view == my_view)[:, :, None], slot_rank[:, :, None] == slot_index[None, None, :]
    )
    strip_table = jnp.sum(jnp.where(slot_match, source_strip[:, :, None], 0), axis=1)
    cross_pairs = projected[:, 4 * head_cols : 6 * head_cols].reshape(
        n_strip, strip_rows, 2 * head_cols
    )
    outgoing = cross_pairs[strip_table]
    received = lax.all_to_all(outgoing, "view", split_axis=0, concat_axis=0, tiled=True)

    def head_block(column_block):
        return projected[:, column_block * head_cols : (column_block + 1) * head_cols].reshape(
            total_rows, heads_here, HEAD_DIM
        )

    self_mix = attend_heads(
        head_block(0), head_block(1), head_block(2), jnp.ones((total_rows,), dtype=bool)
    )
    hidden = projected[:, split_at:]
    my_source = lax.dynamic_index_in_dim(source_view, my_view, 0, keepdims=False)
    my_rank = lax.dynamic_index_in_dim(slot_rank, my_view, 0, keepdims=False)
    picked = received.reshape(n_view * capacity, strip_rows, 2 * head_cols)[
        my_source * capacity + my_rank
    ]
    picked = picked.reshape(n_strip, SLOTS * strip_rows, 2 * head_cols)
    my_count = lax.dynamic_index_in_dim(source_count, my_view, 0, keepdims=False)
    key_valid = jnp.repeat(
        jnp.arange(SLOTS, dtype=jnp.int32)[None, :] < my_count[:, None], strip_rows, axis=1
    )
    cross_heads = projected[:, 3 * head_cols : 4 * head_cols].reshape(
        n_strip, strip_rows, heads_here, HEAD_DIM
    )
    picked_keys = picked[:, :, :head_cols].reshape(
        n_strip, SLOTS * strip_rows, heads_here, HEAD_DIM
    )
    picked_values = picked[:, :, head_cols:].reshape(
        n_strip, SLOTS * strip_rows, heads_here, HEAD_DIM
    )
    cross_mix = jax.vmap(attend_heads)(cross_heads, picked_keys, picked_values, key_valid).reshape(
        total_rows, head_cols
    )
    summed_terms = branch_term(self_mix, self_out)
    summed_terms = summed_terms + branch_term(cross_mix, cross_out)
    summed = lax.psum_scatter(
        (summed_terms + branch_term(hidden, mlp_down)).astype(jnp.bfloat16),
        "strip",
        scatter_dimension=0,
        tiled=True,
    ).astype(jnp.float32)
    return (tokens[0].astype(jnp.float32) + summed).astype(jnp.bfloat16)[None]


def solution(mesh):
    in_specs = (
        P("view", "strip", None),
        P(),
        P(),
        P(None, "strip"),
        P(None, "strip"),
        P(None, "strip"),
        P("strip", None),
        P(None, "strip"),
        P(None, "strip"),
        P(None, "strip"),
        P("strip", None),
        P(None, "strip"),
        P("strip", None),
    )
    out_specs = P("view", "strip", None)
    return jax.shard_map(
        per_device, mesh=mesh, in_specs=in_specs, out_specs=out_specs, check_vma=False
    )
```

profile of v0, /device:TPU:0, one launch (start us, length us, event | category | flops | bytes accessed | tf_op | source)
XLA Modules:
  0.0 192.2 jit_solution(7646376136281344709)
XLA Ops:
  6.5 1.3 fusion.31
  7.9 1.9 fusion.32
  9.8 0.9 copy.73
  10.8 0.5 convert_reduce_fusion
  11.8 2.6 %constant_dynamic-update-slice_fusion.6 = bf16[1536,3840]{1,0:T(8,128)(2,1)} fusion(bf16[1536,384]{1,0:T(8,128)(2,1)} %param.16), kind=kLoop, calls=%fused_computation.57 | loop fusion | bytes 2359296
  14.4 1.3 constant_dynamic-update-slice_fusion.5
  15.7 1.3 constant_dynamic-update-slice_fusion.4
  17.0 1.3 constant_dynamic-update-slice_fusion.3
  18.3 1.3 constant_dynamic-update-slice_fusion.2
  19.6 1.2 constant_dynamic-update-slice_fusion.1
  20.8 2.5 %constant_dynamic-update-slice_fusion = bf16[1536,3840]{1,0:T(8,128)(2,1)} fusion(bf16[1536,3840]{1,0:T(8,128)(2,1)} %constant_dynamic-update-slice_fusion.1, bf16[1536,1536]{1,0:T(8,128)(2,1)S(1)} %bitcast.61), kind=kLoop, calls=%fused_computation.51 | loop fusion | bytes 9437184 | tf_op jit(solution)/shard_map/concatenate | solution.py:59
  23.3 26.4 %all-gather.2.cloned.1.call-done = bf16[512,1536]{1,0:T(8,128)(2,1)} async-done(((bf16[128,1536]{1,0:T(8,128)(2,1)}), bf16[512,1536]{1,0:T(8,128)(2,1)}) %all-gather.2.cloned.1.call-update) | async-done | bytes 1572880 | tf_op jit(solution)/shard_map/all_gather | solution.py:64
  49.7 12.9 %fusion.56 = (bf16[512,3840]{1,0:T(8,128)(2,1)S(1)}, f32[512,3840]{1,0:T(8,128)}) fusion(bf16[512,1536]{1,0:T(8,128)(2,1)} %all-gather.2.cloned.1.call-done, bf16[1536,3840]{1,0:T(8,128)(2,1)} %constant_dynamic-update-slice_fusion), kind=kOutput, calls=%fused_computation.94 | convolution fusion | flops 6041763840 | bytes 25165824 | tf_op jit(solution)/shard_map/dot_general | solution.py:63
  62.6 1.9 copy-done.6
  64.5 3.2 %gather_fusion = bf16[24,128,768]{2,1,0:T(8,128)(2,1)} fusion(bf16[4,128,768]{2,1,0:T(8,128)(2,1)S(1)} %bitcast.56, s32[1024]{0:T(1024)S(1)} %pad_clamp_fusion.1), kind=kCustom, calls=%fused_computation | custom fusion | bytes 9437280 | tf_op jit(solution)/shard_map/gather | solution.py:88
  67.7 4.8 %all-to-all-start = ((bf16[8,3,128,768]{3,2,1,0:T(8,128)(2,1)}), bf16[8,3,128,768]{3,2,1,0:T(8,128)(2,1)}, u32[]{:S(2)}, u32[]{:S(2)}) async-start(bf16[8,3,128,768]{3,2,1,0:T(8,128)(2,1)} %bitcast.57), calls=%async_computation | async-start | bytes 9437184 | tf_op jit(solution)/shard_map/all_to_all | solution.py:89
  73.1 1.5 fusion.54
  75.5 4.8 %fusion.57 = (f32[6,512]{1,0:T(8,128)S(1)}, f32[6,512,512]{1,2,0:T(8,128)}) fusion(bf16[512,6,64]{0,2,1:T(8,128)(2,1)S(1)} %bitcast.66, bf16[512,6,64]{0,2,1:T(8,128)(2,1)S(1)} %bitcast.67), kind=kOutput, calls=%fused_computation.95 | convolution fusion | flops 206045696 | bytes 7090176 | tf_op jit(solution)/shard_map/sub | solution.py:25
  80.3 3.5 %fusion.29 = bf16[6,64,512]{2,1,0:T(8,128)(2,1)S(1)} fusion(bf16[512,6,64]{0,2,1:T(8,128)(2,1)S(1)} %bitcast.65, f32[6,512,512]{1,2,0:T(8,128)} %get-tuple-element.16, f32[6,512]{1,0:T(8,128)S(1)} %get-tuple-element.15), kind=kOutput, calls=%fused_computation.36 | convolution fusion | flops 204668928 | bytes 7090176 | tf_op jit(solution)/shard_map/hqk,khe->qhe/dot_general | solution.py:26
  83.8 2.7 %fusion.59 = f32[512,1536]{1,0:T(8,128)} fusion(bf16[512,384]{0,1:T(8,128)(2,1)S(1)} %bitcast.64, bf16[384,1536]{1,0:T(8,128)(2,1)S(1)} %copy-done), kind=kOutput, calls=%fused_computation.97 | convolution fusion | flops 603979776 | bytes 4718592 | tf_op jit(solution)/shard_map/dot_general | solution.py:33
  86.5 7.7 %fusion.22 = f32[512,1536]{1,0:T(8,128)} fusion(bf16[1536,1536]{1,0:T(8,128)(2,1)} %param.25, f32[512,3840]{1,0:T(8,128)} %get-tuple-element.14), kind=kOutput, calls=%fused_computation.30 | convolution fusion | flops 2422996992 | bytes 11010048 | tf_op jit(solution)/shard_map/dot_general | solution.py:33
  94.2 33.0 %all-to-all-done = bf16[8,3,128,768]{3,2,1,0:T(8,128)(2,1)} async-done(((bf16[8,3,128,768]{3,2,1,0:T(8,128)(2,1)}), bf16[8,3,128,768]{3,2,1,0:T(8,128)(2,1)}, u32[]{:S(2)}, u32[]{:S(2)}) %all-to-all-start) | async-done | bytes 4718624 | tf_op jit(solution)/shard_map/all_to_all | solution.py:89
  127.2 5.4 %gather_fusion.1 = bf16[20,128,768]{2,1,0:T(8,128)(2,1)} fusion(bf16[24,128,768]{2,1,0:T(8,128)(2,1)} %bitcast.10, s32[1024]{0:T(1024)S(1)} %pad_clamp_fusion), kind=kCustom, calls=%fused_computation.1 | custom fusion | bytes 7864400 | tf_op jit(solution)/shard_map/gather | solution.py:102
  132.6 3.9 %fusion.55 = (bf16[4,640,384]{2,1,0:T(8,128)(2,1)}, bf16[4,640,384]{2,1,0:T(8,128)(2,1)S(1)}) fusion(bf16[4,640,768]{2,1,0:T(8,128)(2,1)} %bitcast.58), kind=kLoop, calls=%fused_computation.93 | loop fusion | bytes 7864320 | tf_op jit(solution)/shard_map/slice | solution.py:113
  136.4 2.5 %copy.78 = bf16[4,640,384]{1,2,0:T(8,128)(2,1)} copy(bf16[4,640,384]{2,1,0:T(8,128)(2,1)S(1)} %get-tuple-element.12) | data formatting | bytes 3932160 | tf_op jit(solution)/shard_map/slice | solution.py:116
  138.9 2.8 %copy.80 = bf16[4,640,384]{1,2,0:T(8,128)(2,1)S(1)} copy(bf16[4,640,384]{2,1,0:T(8,128)(2,1)} %get-tuple-element.11) | data formatting | bytes 3932160 | tf_op jit(solution)/shard_map/slice | solution.py:113
  141.7 1.2 fusion.39
  142.9 2.7 %fusion.58 = (f32[4,6,128]{2,1,0:T(8,128)S(1)}, f32[4,6,128,640]{3,2,1,0:T(8,128)S(1)}) fusion(f32[4,6,128,640]{3,2,1,0:T(8,128)S(1)} %fusion.39, pred[4,640]{1,0:T(4,128)(4,1)S(1)} %bitcast.68), kind=kOutput, calls=%fused_computation.96 | output fusion | flops 11797119 | bytes 15743488 | tf_op jit(solution)/shard_map/vmap()/sub | solution.py:25
  145.7 2.1 %fusion.30 = bf16[4,128,6,64]{1,3,2,0:T(8,128)(2,1)S(1)} fusion(bf16[4,640,6,64]{1,3,2,0:T(8,128)(2,1)S(1)} %bitcast.62, f32[4,6,128,640]{3,2,1,0:T(8,128)S(1)} %get-tuple-element.18, f32[4,6,128]{2,1,0:T(8,128)S(1)} %get-tuple-element.17), kind=kOutput, calls=%fused_computation.37 | convolution fusion | flops 255787008 | bytes 10235904 | tf_op jit(solution)/shard_map/vmap(hqk,khe->qhe)/dot_general | solution.py:26
  148.8 2.2 %fusion.21 = bf16[512,1536]{1,0:T(8,128)(2,1)} fusion(f32[512,1536]{1,0:T(8,128)S(1)} %copy-done.4, f32[512,1536]{1,0:T(8,128)S(1)} %copy-done.2, bf16[384,1536]{1,0:T(8,128)(2,1)S(1)} %copy-done.7, bf16[48,8,4,128]{3,2,1,0:T(4,128)(2,1)S(1)} %bitcast.63), kind=kOutput, calls=%fused_computation.29 | convolution fusion | flops 606339072 | bytes 9437184 | tf_op jit(solution)/shard_map/dot_general | solution.py:33
  151.0 32.5 %reduce-scatter.2.cloned.1.call-done = bf16[128,1536]{1,0:T(8,128)(2,1)} async-done(((bf16[512,1536]{1,0:T(8,128)(2,1)}), bf16[128,1536]{1,0:T(8,128)(2,1)}) %reduce-scatter.2.cloned.1.call-update) | async-done | bytes 393232 | tf_op jit(solution)/shard_map/reduce_scatter | solution.py:124
  183.6 1.8 fusion.36
  (61 shorter events, 3.2 us)
Async XLA Ops:
  6.5 77.3 %copy-start = (bf16[384,1536]{1,0:T(8,128)(2,1)S(1)}, bf16[384,1536]{1,0:T(8,128)(2,1)}, u32[]{:S(2)}) copy-start(bf16[384,1536]{1,0:T(8,128)(2,1)} %param.19) | copy-start | bytes 3538948
  6.5 7.9 %copy-start.8 = (bf16[1536,384]{1,0:T(8,128)(2,1)S(1)}, bf16[1536,384]{1,0:T(8,128)(2,1)}, u32[]{:S(2)}) copy-start(bf16[1536,384]{1,0:T(8,128)(2,1)} %param.17) | copy-start | bytes 3538948
  6.5 43.2 %all-gather.2.cloned.1.call-start = ((), (), s32[]{:S(2)}) async-start(), calls=%async_computation.2 | async-start | bytes 1966080 | tf_op jit(solution)/shard_map/all_gather | solution.py:64
  9.8 11.1 %slice-start = ((s8[4718592]{0:T(1024)(128)(4,1)}), s8[524288]{0:T(1024)(128)(4,1)S(1)}, s32[]{:S(2)}) async-start(s8[4718592]{0:T(1024)(128)(4,1)} %bitcast.60), calls=%async_computation.4 | async-start | bytes 1048576
  11.7 4.0 %copy-start.9 = (bf16[1536,384]{1,0:T(8,128)(2,1)S(1)}, bf16[1536,384]{1,0:T(8,128)(2,1)}, u32[]{:S(2)}) copy-start(bf16[1536,384]{1,0:T(8,128)(2,1)} %param.18) | copy-start | bytes 3538948
  11.7 5.3 %copy-start.10 = (bf16[1536,384]{1,0:T(8,128)(2,1)S(1)}, bf16[1536,384]{1,0:T(8,128)(2,1)}, u32[]{:S(2)}) copy-start(bf16[1536,384]{1,0:T(8,128)(2,1)} %param.20) | copy-start | bytes 3538948
  14.4 3.9 %copy-start.11 = (bf16[1536,384]{1,0:T(8,128)(2,1)S(1)}, bf16[1536,384]{1,0:T(8,128)(2,1)}, u32[]{:S(2)}) copy-start(bf16[1536,384]{1,0:T(8,128)(2,1)} %param.21) | copy-start | bytes 3538948
  15.7 3.9 %copy-start.12 = (bf16[1536,384]{1,0:T(8,128)(2,1)S(1)}, bf16[1536,384]{1,0:T(8,128)(2,1)}, u32[]{:S(2)}) copy-start(bf16[1536,384]{1,0:T(8,128)(2,1)} %param.22) | copy-start | bytes 3538948
  15.7 5.1 %slice-start.1 = ((s8[4718592]{0:T(1024)(128)(4,1)}), s8[4194304]{0:T(1024)(128)(4,1)S(1)}, s32[]{:S(2)}) async-start(s8[4718592]{0:T(1024)(128)(4,1)} %bitcast.60), calls=%async_computation.5 | async-start | bytes 8388608
  62.6 1.9 copy-start.6
  67.7 5.0 %copy-start.13 = (s32[8,4]{0,1:T(4,128)S(1)}, s32[8,4]{0,1:T(4,128)}, u32[]{:S(2)}) copy-start(s32[8,4]{0,1:T(4,128)} %param.15) | copy-start | bytes 388
  67.7 59.5 %all-to-all-start = ((bf16[8,3,128,768]{3,2,1,0:T(8,128)(2,1)}), bf16[8,3,128,768]{3,2,1,0:T(8,128)(2,1)}, u32[]{:S(2)}, u32[]{:S(2)}) async-start(bf16[8,3,128,768]{3,2,1,0:T(8,128)(2,1)} %bitcast.57), calls=%async_computation | async-start | bytes 9437184 | tf_op jit(solution)/shard_map/all_to_all | solution.py:89
  72.5 111.1 %reduce-scatter.2.cloned.1.call-start = ((), (), s32[]{:S(2)}) async-start(), calls=%async_computation.3 | async-start | bytes 1966080 | tf_op jit(solution)/shard_map/reduce_scatter | solution.py:124
  142.9 2.7 %copy-start.5 = (bf16[4,640,384]{1,2,0:T(8,128)(2,1)S(1)}, bf16[4,640,384]{1,2,0:T(8,128)(2,1)}, u32[]{:S(2)}) copy-start(bf16[4,640,384]{1,2,0:T(8,128)(2,1)} %copy.78) | copy-start | bytes 5898244
  145.7 2.4 %copy-start.2 = (f32[512,1536]{1,0:T(8,128)S(1)}, f32[512,1536]{1,0:T(8,128)}, u32[]{:S(2)}) copy-start(f32[512,1536]{1,0:T(8,128)} %fusion.59) | copy-start | bytes 9437188
  145.7 2.8 %copy-start.4 = (f32[512,1536]{1,0:T(8,128)S(1)}, f32[512,1536]{1,0:T(8,128)}, u32[]{:S(2)}) copy-start(f32[512,1536]{1,0:T(8,128)} %fusion.22) | copy-start | bytes 9437188
  145.7 3.1 %copy-start.7 = (bf16[384,1536]{1,0:T(8,128)(2,1)S(1)}, bf16[384,1536]{1,0:T(8,128)(2,1)}, u32[]{:S(2)}) copy-start(bf16[384,1536]{1,0:T(8,128)(2,1)} %param.23) | copy-start | bytes 3538948
  148.1 37.3 %copy-start.1 = (bf16[384,1536]{1,0:T(8,128)(2,1)S(1)}, bf16[384,1536]{1,0:T(8,128)(2,1)}, u32[]{:S(2)}) copy-start(bf16[384,1536]{1,0:T(8,128)(2,1)} %param.19) | copy-start | bytes 3538948
  148.8 34.8 %copy-start.3 = (bf16[1,128,1536]{2,1,0:T(8,128)(2,1)S(1)}, bf16[1,128,1536]{2,1,0:T(8,128)(2,1)}, u32[]{:S(2)}) copy-start(bf16[1,128,1536]{2,1,0:T(8,128)(2,1)} %param.13) | copy-start | bytes 1179652
Sparse Core Ops, SparseCore 0:
  9.9 39.7 all-gather.1
  151.2 32.3 reduce-scatter.1
where the time goes:
time: 193 us; the launch traced here: 192 us
  waiting for transfers between devices  91.9 us (48%)
  matrix products  37.1 us (19%)
  local copies, waits for them, and re-layouts  36.1 us (19%)
  between operations  13.6 us (7%)
  other arithmetic  8.5 us (4%)
  starting transfers between devices  4.98 us (3%)
    all_to_all x1, waiting for transfers between devices, per_device(): lax.all_to_all(outgoing, 'view', split_axis=0, concat_axis=0, tiled=True)  33 us
    reduce_scatter x1, waiting for transfers between devices, per_device(): lax.psum_scatter((summed_terms + branch_term(hidden, mlp_down)).astype(jn...  32.5 us
    all_gather x1, waiting for transfers between devices, per_device(): lax.all_gather(normed, 'strip', axis=0, tiled=True)  26.4 us
    dot_general x1, matrix products, per_device(): jnp.dot(lax.all_gather(normed, 'strip', axis=0, tiled=True), stacked, pre...  12.9 us
    dot_general x3, matrix products, branch_term(): return jnp.dot(mixed_rows, weight, preferred_element_type=jnp.float32)  12.6 us
    unnamed x41, local copies, waits for them, and re-layouts  12.6 us
    slice x2, local copies, waits for them, and re-layouts, per_device(): picked[:, :, :head_cols]  6.64 us
    dot_general x2, matrix products, attend_heads(): jnp.einsum('hqk,khe->qhe', weights, value_heads, preferred_element_type=j...  5.53 us
  transfers between devices with their start and end apart: 3, of which 3 were waited for; matrix products, arithmetic and copies ran while one was open for 18% of the time, Pallas kernels for 0%

commit v1 on v0

v1 whole, which is shorter than its diff:
```python
import functools
import math

import jax
import jax.numpy as jnp
from jax import lax
from jax.experimental import pallas as pl
from jax.experimental.pallas import tpu as pltpu
from jax.sharding import PartitionSpec as P

HEAD_DIM = 64
LANES = 128
MESH = pl.DeviceIdType.MESH
F32 = jnp.float32
BF16 = jnp.bfloat16


def dot(a, b):
    return jnp.dot(a, b, preferred_element_type=F32)


def dot_nt(a, b):
    return lax.dot_general(a, b, (((1,), (1,)), ((), ())), preferred_element_type=F32)


def attend(q, keys, values, bias):
    cols = q.shape[1]
    parts = []
    for lo in range(0, cols, LANES):
        hi = min(lo + LANES, cols)
        q_block = q[:, lo:hi] * jnp.asarray(1.0 / math.sqrt(HEAD_DIM), BF16)
        k_block, v_block = keys(lo, hi), values(lo, hi)
        lane = lax.broadcasted_iota(jnp.int32, q_block.shape, 1)
        result = None
        for head in range((hi - lo) // HEAD_DIM):
            inside = jnp.logical_and(lane >= head * HEAD_DIM, lane < (head + 1) * HEAD_DIM)
            scores = dot_nt(jnp.where(inside, q_block, jnp.zeros_like(q_block)), k_block)
            if bias is not None:
                scores = scores + bias
            top = jnp.max(scores, axis=-1, keepdims=True)
            weights = jnp.exp(scores - top)
            total = jnp.sum(weights, axis=-1, keepdims=True)
            mixed = dot(weights.astype(BF16), v_block) * (1.0 / total)
            result = mixed if result is None else jnp.where(inside, mixed, result)
        parts.append(result.astype(BF16))
    return parts[0] if len(parts) == 1 else jnp.concatenate(parts, axis=1)


def kernel(
    n_view,
    n_strip,
    slots,
    ids,
    counts,
    tokens,
    w_sq,
    w_sk,
    w_sv,
    w_so,
    w_cq,
    w_ck,
    w_cv,
    w_co,
    w_up,
    w_down,
    out,
    wa,
    wo,
    wm,
    md,
    nbuf,
    proj,
    kv,
    kbuf,
    acc,
    rs_send,
    rs_recv,
    w_sem,
    n_send,
    n_recv,
    kv_send,
    fwd_send,
    kv_recv,
    rs_ssem,
    rs_rsem,
):
    v = lax.axis_index("view")
    z = lax.axis_index("strip")
    n_chip = n_view // 2
    chip, core = v // 2, v % 2
    mate = chip * 2 + 1 - core
    rows = tokens.shape[1]
    hc = w_sq.shape[1]
    n_up, _, up = wm.shape
    has_left, has_right = z > 0, z < n_strip - 1

    loads = []

    def load(src, dst):
        copy = pltpu.make_async_copy(src, dst, w_sem.at[len(loads)])
        copy.start()
        loads.append(copy)

    load(w_ck, wa.at[4])
    load(w_cv, wa.at[5])
    load(w_sq, wa.at[0])
    load(w_sk, wa.at[1])
    load(w_sv, wa.at[2])
    load(w_cq, wa.at[3])
    for j in range(n_up):
        load(w_up.at[:, pl.ds(j * up, up)], wm.at[j])
    for j in range(n_up):
        load(w_down.at[pl.ds(j * up, up)], md.at[j])
    load(w_so, wo.at[0])
    load(w_co, wo.at[1])

    barrier = pltpu.get_barrier_semaphore()

    def greet(view, strip):
        pl.semaphore_signal(barrier, inc=1, device_id=(view, strip), device_id_type=MESH)

    peers = [lax.rem(chip + o, n_chip) * 2 + core for o in range(1, n_chip)]
    for p in peers:
        greet(p, z)
    greet(mate, z)

    @pl.when(has_left)
    def _():
        greet(v, z - 1)

    @pl.when(has_right)
    def _():
        greet(v, z + 1)

    wide = tokens[0].astype(F32)
    nbuf[z] = (wide * lax.rsqrt(jnp.mean(wide * wide, axis=-1, keepdims=True) + 1e-06)).astype(BF16)
    pl.semaphore_wait(
        barrier, n_chip + jnp.where(has_left, 1, 0) + jnp.where(has_right, 1, 0)
    )

    def n_copy(b, side):
        return pltpu.make_async_remote_copy(
            src_ref=nbuf.at[b],
            dst_ref=nbuf.at[b],
            send_sem=n_send.at[side, b],
            recv_sem=n_recv.at[b],
            device_id=(v, z + (2 * side - 1)),
            device_id_type=MESH,
        )

    def kv_copy(view, t, to, sem):
        index = view * n_strip + t
        return pltpu.make_async_remote_copy(
            src_ref=kv.at[index],
            dst_ref=kv.at[index],
            send_sem=sem,
            recv_sem=kv_recv.at[index],
            device_id=(to, z),
            device_id_type=MESH,
        )

    def share(t):
        for o, p in enumerate(peers):
            kv_copy(v, t, p, kv_send.at[o, t]).start()
        kv_copy(v, t, mate, kv_send.at[n_chip - 1, t]).start()

    def forward(t):
        for o, p in enumerate(peers):
            kv_copy(p, t, mate, fwd_send.at[o, t]).wait_recv()
            kv_copy(p, t, mate, fwd_send.at[o, t]).start()

    def project_kv(b):
        x = nbuf[b]
        index = v * n_strip + b
        kv[index, :, 0:hc] = dot(x, wa[4]).astype(BF16)
        kv[index, :, hc : 2 * hc] = dot(x, wa[5]).astype(BF16)
        share(b)

    def project_rest(b):
        def one(i, carry):
            proj[i, b] = dot(nbuf[b], wa[i]).astype(BF16)
            return carry

        lax.fori_loop(0, 4, one, 0)

        def mlp(j, carry):
            hidden = jax.nn.gelu(dot(nbuf[b], wm[j])).astype(BF16)
            term = dot(hidden, md[j])

            @pl.when(j == 0)
            def _():
                acc[b] = term

            @pl.when(j > 0)
            def _():
                acc[b] = acc[b] + term

            return carry

        lax.fori_loop(0, n_up, mlp, 0)

    def at_distance(d, fn):
        @pl.when(z - d >= 0)
        def _():
            fn(z - d)

        @pl.when(z + d < n_strip)
        def _():
            fn(z + d)

    @pl.when(has_left)
    def _():
        n_copy(z, 0).start()

    @pl.when(has_right)
    def _():
        n_copy(z, 1).start()

    for copy in loads[:2]:
        copy.wait()
    project_kv(z)
    for copy in loads[2:]:
        copy.wait()
    project_rest(z)

    def gather_step(d, carry):
        @pl.when(z - d >= 0)
        def _():
            n_copy(z - d, 1).wait_recv()

            @pl.when(has_right)
            def _():
                n_copy(z - d, 1).start()

        @pl.when(z + d < n_strip)
        def _():
            n_copy(z + d, 0).wait_recv()

            @pl.when(has_left)
            def _():
                n_copy(z + d, 0).start()

        def both(fn):
            def one(side, c):
                b = z + (2 * side - 1) * d

                @pl.when(jnp.logical_and(b >= 0, b < n_strip))
                def _():
                    fn(b)

                return c

            lax.fori_loop(0, 2, one, 0)

        both(project_kv)
        both(project_rest)

        @pl.when(d == 1)
        def _():
            forward(z)

        @pl.when(d > 1)
        def _():
            both_prev = d - 1
            at_distance(both_prev, forward)

        return carry

    lax.fori_loop(1, n_strip, gather_step, 0)

    def self_strip(s, carry):
        def columns(i):
            return lambda lo, hi: proj[i, :, :, lo:hi].reshape(n_strip * rows, hi - lo)

        mixed = attend(proj[0, s], columns(1), columns(2), None)
        acc[s] = acc[s] + dot(mixed, wo[0])
        return carry

    lax.fori_loop(0, n_strip, self_strip, 0)

    at_distance(n_strip - 1, forward)

    def from_mate(t, carry):
        kv_copy(mate, t, mate, fwd_send.at[0, t]).wait_recv()
        for p in peers:
            kv_copy(p + 1 - 2 * core, t, mate, fwd_send.at[0, t]).wait_recv()
        return carry

    lax.fori_loop(0, n_strip, from_mate, 0)

    def rs_copy(s, side):
        slot = jnp.where(jnp.logical_and(side == 0, s == z - 1), n_strip, s)
        return pltpu.make_async_remote_copy(
            src_ref=rs_send.at[s],
            dst_ref=rs_recv.at[slot],
            send_sem=rs_ssem.at[s],
            recv_sem=rs_rsem.at[slot],
            device_id=(v, z + (2 * side - 1)),
            device_id_type=MESH,
        )

    def rs_wait(slot, side):
        pltpu.make_async_remote_copy(
            src_ref=rs_send.at[0],
            dst_ref=rs_recv.at[slot],
            send_sem=rs_ssem.at[0],
            recv_sem=rs_rsem.at[slot],
            device_id=(v, z + (2 * side - 1)),
            device_id_type=MESH,
        ).wait_recv()

    def nth(i):
        low = n_strip - 1 - i
        low = jnp.where(low > z, low, low - 1)
        high = jnp.where(i < z, i, i + 1)
        return jnp.where(i == n_strip - 1, z, jnp.where(z < n_strip // 2, low, high))

    def cross_strip(i, carry):
        s = nth(i)
        base = (v * n_strip + s) * slots
        for k in range(slots):
            kbuf[k] = kv[ids[base + k]]
        count = counts[v * n_strip + s]
        column = lax.broadcasted_iota(jnp.int32, (1, slots * rows), 1)
        bias = jnp.where(column < count * rows, 0.0, -1e30).astype(F32)

        def columns(start):
            return lambda lo, hi: kbuf[:, :, start + lo : start + hi].reshape(slots * rows, hi - lo)

        mixed = attend(proj[3, s], columns(0), columns(hc), bias)
        acc[s] = acc[s] + dot(mixed, wo[1])

        @pl.when(jnp.logical_and(s > z, z == 0))
        def _():
            rs_send[s] = acc[s].astype(BF16)
            rs_copy(s, 1).start()

        @pl.when(jnp.logical_and(s < z, z == n_strip - 1))
        def _():
            rs_send[s] = acc[s].astype(BF16)
            rs_copy(s, 0).start()

        return carry

    lax.fori_loop(0, n_strip, cross_strip, 0)

    def pass_on(i, carry):
        s = nth(i)

        @pl.when(jnp.logical_and(s > z, has_left))
        def _():
            rs_wait(s, 1)
            rs_send[s] = (acc[s] + rs_recv[s].astype(F32)).astype(BF16)
            rs_copy(s, 1).start()

        @pl.when(jnp.logical_and(s < z, has_right))
        def _():
            rs_wait(s, 0)
            rs_send[s] = (acc[s] + rs_recv[s].astype(F32)).astype(BF16)
            rs_copy(s, 0).start()

        return carry

    lax.fori_loop(0, n_strip - 1, pass_on, 0)

    @pl.when(has_left)
    def _():
        rs_wait(z, 1)
        acc[z] = acc[z] + rs_recv[z].astype(F32)

    @pl.when(has_right)
    def _():
        rs_wait(n_strip, 0)
        acc[z] = acc[z] + rs_recv[n_strip].astype(F32)

    out[0] = (tokens[0].astype(F32) + acc[z]).astype(BF16)

    def settle(t, carry):
        @pl.when(jnp.logical_and(has_left, t >= z))
        def _():
            n_copy(t, 0).wait_send()

        @pl.when(jnp.logical_and(has_right, t <= z))
        def _():
            n_copy(t, 1).wait_send()

        for o, p in enumerate(peers):
            kv_copy(v, t, p, kv_send.at[o, t]).wait_send()
            kv_copy(p, t, mate, fwd_send.at[o, t]).wait_send()
        kv_copy(v, t, mate, kv_send.at[n_chip - 1, t]).wait_send()

        @pl.when(t > z)
        def _():
            rs_copy(t, 1).wait_send()

        @pl.when(t < z)
        def _():
            rs_copy(t, 0).wait_send()

        return carry

    lax.fori_loop(0, n_strip, settle, 0)


def per_device(n_view, n_strip, tokens, source_ids, source_count, *weights):
    rows, width = tokens.shape[1:]
    hc = weights[0].shape[1]
    hidden = weights[-2].shape[1]
    slots = source_ids.shape[2]
    up = next(u for u in (384, 256, 128, hidden) if hidden % u == 0)
    n_up = hidden // up
    n_chip = n_view // 2
    dma = pltpu.SemaphoreType.DMA
    smem = pl.BlockSpec(memory_space=pltpu.SMEM)
    vmem = pl.BlockSpec(memory_space=pltpu.VMEM)
    hbm = pl.BlockSpec(memory_space=pl.ANY)
    return pl.pallas_call(
        functools.partial(kernel, n_view, n_strip, slots),
        out_shape=jax.ShapeDtypeStruct(tokens.shape, tokens.dtype),
        in_specs=[smem, smem, vmem] + [hbm] * len(weights),
        out_specs=vmem,
        scratch_shapes=[
            pltpu.VMEM((6, width, hc), BF16),
            pltpu.VMEM((2, hc, width), BF16),
            pltpu.VMEM((n_up, width, up), BF16),
            pltpu.VMEM((n_up, up, width), BF16),
            pltpu.VMEM((n_strip, rows, width), BF16),
            pltpu.VMEM((4, n_strip, rows, hc), BF16),
            pltpu.VMEM((n_view * n_strip, rows, 2 * hc), BF16),
            pltpu.VMEM((slots, rows, 2 * hc), BF16),
            pltpu.VMEM((n_strip, rows, width), F32),
            pltpu.VMEM((n_strip, rows, width), BF16),
            pltpu.VMEM((n_strip + 1, rows, width), BF16),
            dma((8 + 2 * n_up,)),
            dma((2, n_strip)),
            dma((n_strip,)),
            dma((n_chip, n_strip)),
            dma((n_chip, n_strip)),
            dma((n_view * n_strip,)),
            dma((n_strip,)),
            dma((n_strip + 1,)),
        ],
        compiler_params=pltpu.CompilerParams(
            collective_id=0, has_side_effects=True, vmem_limit_bytes=60 * 1024 * 1024
        ),
    )(source_ids.reshape(-1), source_count.reshape(-1), tokens, *weights)


def solution(mesh):
    column, row = P(None, "strip"), P("strip", None)
    in_specs = (
        P("view", "strip", None),
        P(),
        P(),
        column,
        column,
        column,
        row,
        column,
        column,
        column,
        row,
        column,
        row,
    )
    return jax.shard_map(
        functools.partial(per_device, mesh.shape["view"], mesh.shape["strip"]),
        mesh=mesh,
        in_specs=in_specs,
        out_specs=P("view", "strip", None),
        check_vma=False,
    )
```

time: 193 us -> 88.2 us (0.46)
  waiting for transfers between devices: 91.9 us -> 0 us
  Pallas kernels: 0 us -> 82.5 us
  matrix products: 37.1 us -> 0 us
  local copies, waits for them, and re-layouts: 36.1 us -> 4.65 us
  between operations: 13.6 us -> 0.01 us
  other arithmetic: 8.5 us -> 0 us
  starting transfers between devices: 4.98 us -> 0 us
    pallas_call x0 -> x1, Pallas kernels: none -> 82.5 us  [per_device(): pl.pallas_call(functools.partial(kernel, n_view, n_strip, slots), out_sha...]
    all_to_all x1 -> x0, waiting for transfers between devices: 33 us -> none  [per_device(): lax.all_to_all(outgoing, 'view', split_axis=0, concat_axis=0, tiled=True)]
    reduce_scatter x1 -> x0, waiting for transfers between devices: 32.5 us -> none  [per_device(): lax.psum_scatter((summed_terms + branch_term(hidden, mlp_down)).astype(jn...]
    dot_general x7 -> x0, matrix products: 32.3 us -> none  [the longest x1 12.9 us: per_device(): jnp.dot(lax.all_gather(normed, 'strip', axis=0, tiled=True), stacked, pre...]
    all_gather x1 -> x0, waiting for transfers between devices: 26.4 us -> none  [per_device(): lax.all_gather(normed, 'strip', axis=0, tiled=True)]
    slice x9 -> x0, local copies, waits for them, and re-layouts: 11.4 us -> none  [the longest x2 6.64 us: per_device(): picked[:, :, :head_cols]]
    unnamed x41 -> x3, local copies, waits for them, and re-layouts: 12.6 us -> 3.32 us
    gather x2 -> x0, local copies, waits for them, and re-layouts: 8.54 us -> none  [the longest x1 5.36 us: per_device(): received.reshape(n_view * capacity, strip_rows, 2 * head_cols)]
  transfers between devices with their start and end apart: 3 -> 0, of which waited for: 3 -> 0; matrix products, arithmetic and copies ran while one was open for 18% -> 0% of each run, Pallas kernels for 0% -> 0%
where the time goes in v1:
time: 88.2 us; the launch traced here: 87.2 us
  Pallas kernels  82.5 us (94%)
  local copies, waits for them, and re-layouts  4.65 us (5%)
    pallas_call x1, Pallas kernels, per_device(): pl.pallas_call(functools.partial(kernel, n_view, n_strip, slots), out_sha...  82.5 us
    unnamed x3, local copies, waits for them, and re-layouts  3.32 us

profile of v1, /device:TPU:0, one launch (start us, length us, event | category | flops | bytes accessed | tf_op | source)
XLA Modules:
  0.0 87.2 jit_solution(12528790718713934553)
XLA Ops:
  0.0 0.8 copy.16
  0.8 0.7 reshape.7.counts
  1.4 0.8 copy.15
  2.2 0.7 reshape.6.ids
  2.9 82.5 %shard_map.127 = bf16[1,128,1536]{2,1,0:T(8,128)(2,1)} custom-call(s32[160]{0:T(256)} %reshape.6.ids, s32[32]{0:T(128)} %reshape.7.counts, bf16[1,128,1536]{2,1,0:T(8,128)(2,1)} %tokens.1, bf16[1536,384]{1,0:T(8,128)(2,1)} %w_sq.1, bf16[1536,384]{1,0:T(8,128)(2,1)} %w_sk.1, bf16[1536,384]{1,0:T(8,128)(2,1)} %w_sv.1, bf16[384,1536]{1,0:T(8,128)(2,1)} %w_so.1, ...), custom_call_target="tpu_custom_call" | custom-call | tf_op jit(solution)/shard_map/pallas_call | solution.py:417
  85.4 1.8 %copy.18 = bf16[1,128,1536]{2,1,0:T(8,128)(2,1)} copy(bf16[1,128,1536]{2,1,0:T(8,128)(2,1)} %shard_map.127) | data formatting | bytes 786432

commit v2 on v1

--- a/solution.py
+++ b/solution.py
@@ -50,8 +50,8 @@
     n_view,
     n_strip,
     slots,
-    ids,
-    counts,
+    ids_in,
+    counts_in,
     tokens,
     w_sq,
     w_sk,
@@ -64,6 +64,8 @@
     w_up,
     w_down,
     out,
+    ids,
+    counts,
     wa,
     wo,
     wm,
@@ -80,6 +82,7 @@
     n_recv,
     kv_send,
     fwd_send,
+    rel_send,
     kv_recv,
     rs_ssem,
     rs_rsem,
@@ -103,6 +106,129 @@
 
     load(w_ck, wa.at[4])
     load(w_cv, wa.at[5])
+
+    barrier = pltpu.get_barrier_semaphore()
+
+    def greet(view, strip):
+        pl.semaphore_signal(barrier, inc=1, device_id=(view, strip), device_id_type=MESH)
+
+    relay = n_chip == 4
+    if relay:
+        near_x = chip + 1 - 2 * (chip % 2)
+        near_y = lax.rem(chip + 2, 4)
+        peers = [near_x * 2 + core, near_y * 2 + core]
+        far = lax.rem(near_x + 2, 4) * 2 + core
+        others = peers + [far]
+    else:
+        peers = [lax.rem(chip + o, n_chip) * 2 + core for o in range(1, n_chip)]
+        others = peers
+    for p in peers:
+        greet(p, z)
+    greet(mate, z)
+
+    @pl.when(has_left)
+    def _():
+        greet(v, z - 1)
+
+    @pl.when(has_right)
+    def _():
+        greet(v, z + 1)
+
+    wide = tokens[0].astype(F32)
+    nbuf[z] = (wide * lax.rsqrt(jnp.mean(wide * wide, axis=-1, keepdims=True) + 1e-06)).astype(BF16)
+    pl.semaphore_wait(
+        barrier, len(peers) + 1 + jnp.where(has_left, 1, 0) + jnp.where(has_right, 1, 0)
+    )
+
+    def n_copy(b, side):
+        return pltpu.make_async_remote_copy(
+            src_ref=nbuf.at[b],
+            dst_ref=nbuf.at[b],
+            send_sem=n_send.at[side, b],
+            recv_sem=n_recv.at[b],
+            device_id=(v, z + (2 * side - 1)),
+            device_id_type=MESH,
+        )
+
+    def kv_copy(view, t, to, sem, half=None):
+        index = view * n_strip + t
+        part = kv.at[index]
+        if half is not None:
+            part = kv.at[index, pl.ds(half * (rows // 2), rows // 2)]
+        return pltpu.make_async_remote_copy(
+            src_ref=part,
+            dst_ref=part,
+            send_sem=sem,
+            recv_sem=kv_recv.at[index, half or 0],
+            device_id=(to, z),
+            device_id_type=MESH,
+        )
+
+    def share(t):
+        for o, p in enumerate(peers):
+            kv_copy(v, t, p, kv_send.at[o, t]).start()
+        kv_copy(v, t, mate, kv_send.at[n_chip - 1, t]).start()
+
+    def forward(t):
+        for o, p in enumerate(peers):
+            kv_copy(p, t, mate, fwd_send.at[o, t]).wait_recv()
+            if relay:
+                kv_copy(p, t, peers[1 - o], rel_send.at[o, t], o).start()
+            kv_copy(p, t, mate, fwd_send.at[o, t]).start()
+
+    def forward_far(t):
+        if relay:
+            for half in range(2):
+                kv_copy(far, t, mate, fwd_send.at[2, t], half).wait_recv()
+            kv_copy(far, t, mate, fwd_send.at[2, t]).start()
+
+    def project_kv(b):
+        x = nbuf[b]
+        index = v * n_strip + b
+        kv[index, :, 0:hc] = dot(x, wa[4]).astype(BF16)
+        kv[index, :, hc : 2 * hc] = dot(x, wa[5]).astype(BF16)
+        share(b)
+
+    def project_rest(b):
+        def one(i, carry):
+            proj[i, b] = dot(nbuf[b], wa[i]).astype(BF16)
+            return carry
+
+        lax.fori_loop(0, 4, one, 0)
+
+        def mlp(j, carry):
+            hidden = jax.nn.gelu(dot(nbuf[b], wm[j])).astype(BF16)
+            term = dot(hidden, md[j])
+
+            @pl.when(j == 0)
+            def _():
+                acc[b] = term
+
+            @pl.when(j > 0)
+            def _():
+                acc[b] = acc[b] + term
+
+            return carry
+
+        lax.fori_loop(0, n_up, mlp, 0)
+
+    def at_distance(d, fn):
+        @pl.when(z - d >= 0)
+        def _():
+            fn(z - d)
+
+        @pl.when(jnp.logical_and(z + d < n_strip, d > 0))
+        def _():
+            fn(z + d)
+
+    @pl.when(has_left)
+    def _():
+        n_copy(z, 0).start()
+
+    @pl.when(has_right)
+    def _():
+        n_copy(z, 1).start()
+
     load(w_sq, wa.at[0])
     load(w_sk, wa.at[1])
     load(w_sv, wa.at[2])
@@ -113,108 +239,8 @@
         load(w_down.at[pl.ds(j * up, up)], md.at[j])
     load(w_so, wo.at[0])
     load(w_co, wo.at[1])
-
-    barrier = pltpu.get_barrier_semaphore()
-
-    def greet(view, strip):
-        pl.semaphore_signal(barrier, inc=1, device_id=(view, strip), device_id_type=MESH)
-
-    peers = [lax.rem(chip + o, n_chip) * 2 + core for o in range(1, n_chip)]
-    for p in peers:
-        greet(p, z)
-    greet(mate, z)
-
-    @pl.when(has_left)
-    def _():
-        greet(v, z - 1)
-
-    @pl.when(has_right)
-    def _():
-        greet(v, z + 1)
-
-    wide = tokens[0].astype(F32)
-    nbuf[z] = (wide * lax.rsqrt(jnp.mean(wide * wide, axis=-1, keepdims=True) + 1e-06)).astype(BF16)
-    pl.semaphore_wait(
-        barrier, n_chip + jnp.where(has_left, 1, 0) + jnp.where(has_right, 1, 0)
-    )
-
-    def n_copy(b, side):
-        return pltpu.make_async_remote_copy(
-            src_ref=nbuf.at[b],
-            dst_ref=nbuf.at[b],
-            send_sem=n_send.at[side, b],
-            recv_sem=n_recv.at[b],
-            device_id=(v, z + (2 * side - 1)),
-            device_id_type=MESH,
-        )
-
-    def kv_copy(view, t, to, sem):
-        index = view * n_strip + t
-        return pltpu.make_async_remote_copy(
-            src_ref=kv.at[index],
-            dst_ref=kv.at[index],
-            send_sem=sem,
-            recv_sem=kv_recv.at[index],
-            device_id=(to, z),
-            device_id_type=MESH,
-        )
-
-    def share(t):
-        for o, p in enumerate(peers):
-            kv_copy(v, t, p, kv_send.at[o, t]).start()
-        kv_copy(v, t, mate, kv_send.at[n_chip - 1, t]).start()
-
-    def forward(t):
-        for o, p in enumerate(peers):
-            kv_copy(p, t, mate, fwd_send.at[o, t]).wait_recv()
-            kv_copy(p, t, mate, fwd_send.at[o, t]).start()
-
-    def project_kv(b):
-        x = nbuf[b]
-        index = v * n_strip + b
-        kv[index, :, 0:hc] = dot(x, wa[4]).astype(BF16)
-        kv[index, :, hc : 2 * hc] = dot(x, wa[5]).astype(BF16)
-        share(b)
-
-    def project_rest(b):
-        def one(i, carry):
-            proj[i, b] = dot(nbuf[b], wa[i]).astype(BF16)
-            return carry
-
-        lax.fori_loop(0, 4, one, 0)
-
-        def mlp(j, carry):
-            hidden = jax.nn.gelu(dot(nbuf[b], wm[j])).astype(BF16)
-            term = dot(hidden, md[j])
-
-            @pl.when(j == 0)
-            def _():
-                acc[b] = term
-
-            @pl.when(j > 0)
-            def _():
-                acc[b] = acc[b] + term
-
-            return carry
-
-        lax.fori_loop(0, n_up, mlp, 0)
-
-    def at_distance(d, fn):
-        @pl.when(z - d >= 0)
-        def _():
-            fn(z - d)
-
-        @pl.when(z + d < n_strip)
-        def _():
-            fn(z + d)
-
-    @pl.when(has_left)
-    def _():
-        n_copy(z, 0).start()
-
-    @pl.when(has_right)
-    def _():
-        n_copy(z, 1).start()
+    load(ids_in, ids)
+    load(counts_in, counts)
 
     for copy in loads[:2]:
         copy.wait()
@@ -253,20 +279,13 @@
             lax.fori_loop(0, 2, one, 0)
 
         both(project_kv)
+        at_distance(d - 1, forward)
         both(project_rest)
-
-        @pl.when(d == 1)
-        def _():
-            forward(z)
-
-        @pl.when(d > 1)
-        def _():
-            both_prev = d - 1
-            at_distance(both_prev, forward)
-
+        at_distance(d - 1, forward_far)
         return carry
 
     lax.fori_loop(1, n_strip, gather_step, 0)
+    at_distance(n_strip - 1, forward)
 
     def self_strip(s, carry):
         def columns(i):
@@ -278,11 +297,11 @@
 
     lax.fori_loop(0, n_strip, self_strip, 0)
 
-    at_distance(n_strip - 1, forward)
+    at_distance(n_strip - 1, forward_far)
 
     def from_mate(t, carry):
         kv_copy(mate, t, mate, fwd_send.at[0, t]).wait_recv()
-        for p in peers:
+        for p in others:
             kv_copy(p + 1 - 2 * core, t, mate, fwd_send.at[0, t]).wait_recv()
         return carry
 
@@ -317,10 +336,9 @@
 
     def cross_strip(i, carry):
         s = nth(i)
-        base = (v * n_strip + s) * slots
         for k in range(slots):
-            kbuf[k] = kv[ids[base + k]]
-        count = counts[v * n_strip + s]
+            kbuf[k] = kv[ids[k, s, v]]
+        count = counts[s, v]
         column = lax.broadcasted_iota(jnp.int32, (1, slots * rows), 1)
         bias = jnp.where(column < count * rows, 0.0, -1e30).astype(F32)
 
@@ -342,7 +360,6 @@
 
         return carry
 
-    lax.fori_loop(0, n_strip, cross_strip, 0)
 
     def pass_on(i, carry):
         s = nth(i)
@@ -361,7 +378,17 @@
 
         return carry
 
-    lax.fori_loop(0, n_strip - 1, pass_on, 0)
+    def sum_step(i, carry):
+        cross_strip(i, 0)
+
+        @pl.when(i >= 2)
+        def _():
+            pass_on(i - 2, 0)
+
+        return carry
+
+    lax.fori_loop(0, n_strip, sum_step, 0)
+    lax.fori_loop(n_strip - 2, n_strip - 1, pass_on, 0)
 
     @pl.when(has_left)
     def _():
@@ -387,6 +414,10 @@
         for o, p in enumerate(peers):
             kv_copy(v, t, p, kv_send.at[o, t]).wait_send()
             kv_copy(p, t, mate, fwd_send.at[o, t]).wait_send()
+            if relay:
+                kv_copy(p, t, mate, rel_send.at[o, t], o).wait_send()
+        if relay:
+            kv_copy(far, t, mate, fwd_send.at[2, t]).wait_send()
         kv_copy(v, t, mate, kv_send.at[n_chip - 1, t]).wait_send()
 
         @pl.when(t > z)
@@ -411,15 +442,16 @@
     n_up = hidden // up
     n_chip = n_view // 2
     dma = pltpu.SemaphoreType.DMA
-    smem = pl.BlockSpec(memory_space=pltpu.SMEM)
     vmem = pl.BlockSpec(memory_space=pltpu.VMEM)
     hbm = pl.BlockSpec(memory_space=pl.ANY)
     return pl.pallas_call(
         functools.partial(kernel, n_view, n_strip, slots),
         out_shape=jax.ShapeDtypeStruct(tokens.shape, tokens.dtype),
-        in_specs=[smem, smem, vmem] + [hbm] * len(weights),
+        in_specs=[hbm, hbm, vmem] + [hbm] * len(weights),
         out_specs=vmem,
         scratch_shapes=[
+            pltpu.SMEM(source_ids.shape[::-1], jnp.int32),
+            pltpu.SMEM(source_count.shape[::-1], jnp.int32),
             pltpu.VMEM((6, width, hc), BF16),
             pltpu.VMEM((2, hc, width), BF16),
             pltpu.VMEM((n_up, width, up), BF16),
@@ -431,19 +463,20 @@
             pltpu.VMEM((n_strip, rows, width), F32),
             pltpu.VMEM((n_strip, rows, width), BF16),
             pltpu.VMEM((n_strip + 1, rows, width), BF16),
-            dma((8 + 2 * n_up,)),
+            dma((10 + 2 * n_up,)),
             dma((2, n_strip)),
             dma((n_strip,)),
             dma((n_chip, n_strip)),
             dma((n_chip, n_strip)),
-            dma((n_view * n_strip,)),
+            dma((2, n_strip)),
+            dma((n_view * n_strip, 2)),
             dma((n_strip,)),
             dma((n_strip + 1,)),
         ],
         compiler_params=pltpu.CompilerParams(
             collective_id=0, has_side_effects=True, vmem_limit_bytes=60 * 1024 * 1024
         ),
-    )(source_ids.reshape(-1), source_count.reshape(-1), tokens, *weights)
+    )(source_ids.transpose(2, 1, 0), source_count.T, tokens, *weights)
 
 
 def solution(mesh):

time: 88.2 us -> 93 us (1.054)
  Pallas kernels: 82.5 us -> 91 us
  local copies, waits for them, and re-layouts: 4.65 us -> 1.77 us
    pallas_call x1, Pallas kernels: 82.5 us -> 91 us  [per_device(): pl.pallas_call(functools.partial(kernel, n_view, n_strip, slots), out_sha...]
    unnamed x3 -> x1, local copies, waits for them, and re-layouts: 3.32 us -> 1.77 us
    reshape x2 -> x0, local copies, waits for them, and re-layouts: 1.33 us -> none  [the longest x1 0.68 us: per_device(): source_ids.reshape(-1)]
where the time goes in v2:
time: 93 us; the launch traced here: 92.8 us
  Pallas kernels  91 us (98%)
  local copies, waits for them, and re-layouts  1.77 us (2%)
    pallas_call x1, Pallas kernels, per_device(): pl.pallas_call(functools.partial(kernel, n_view, n_strip, slots), out_sha...  91 us

profile of v2, /device:TPU:0, one launch (start us, length us, event | category | flops | bytes accessed | tf_op | source)
XLA Modules:
  0.0 92.8 jit_solution(7552080132039227939)
XLA Ops:
  0.0 91.0 %shard_map.127 = bf16[1,128,1536]{2,1,0:T(8,128)(2,1)} custom-call(s32[5,4,8]{2,1,0:T(4,128)} %bitcast.2, s32[4,8]{1,0:T(4,128)} %bitcast.3, bf16[1,128,1536]{2,1,0:T(8,128)(2,1)} %tokens.1, bf16[1536,384]{1,0:T(8,128)(2,1)} %w_sq.1, bf16[1536,384]{1,0:T(8,128)(2,1)} %w_sk.1, bf16[1536,384]{1,0:T(8,128)(2,1)} %w_sv.1, bf16[384,1536]{1,0:T(8,128)(2,1)} %w_so.1, ...), custom_call_target="tpu_custom_call" | custom-call | tf_op jit(solution)/shard_map/pallas_call | solution.py:447
  91.1 1.8 %copy.15 = bf16[1,128,1536]{2,1,0:T(8,128)(2,1)} copy(bf16[1,128,1536]{2,1,0:T(8,128)(2,1)} %shard_map.127) | data formatting | bytes 786432

commit v3 on v1

--- a/solution.py
+++ b/solution.py
@@ -50,8 +50,8 @@
     n_view,
     n_strip,
     slots,
-    ids,
-    counts,
+    ids_in,
+    counts_in,
     tokens,
     w_sq,
     w_sk,
@@ -64,6 +64,8 @@
     w_up,
     w_down,
     out,
+    ids,
+    counts,
     wa,
     wo,
     wm,
@@ -92,6 +94,7 @@
     rows = tokens.shape[1]
     hc = w_sq.shape[1]
     n_up, _, up = wm.shape
+    pair = wa.shape[2] // hc
     has_left, has_right = z > 0, z < n_strip - 1
 
     loads = []
@@ -101,18 +104,14 @@
         copy.start()
         loads.append(copy)
 
-    load(w_ck, wa.at[4])
-    load(w_cv, wa.at[5])
-    load(w_sq, wa.at[0])
-    load(w_sk, wa.at[1])
-    load(w_sv, wa.at[2])
-    load(w_cq, wa.at[3])
-    for j in range(n_up):
-        load(w_up.at[:, pl.ds(j * up, up)], wm.at[j])
-    for j in range(n_up):
-        load(w_down.at[pl.ds(j * up, up)], md.at[j])
-    load(w_so, wo.at[0])
-    load(w_co, wo.at[1])
+    def load_columns(src, i):
+        if pair == 2:
+            load(src, wa.at[i // 2, :, pl.ds(i % 2 * hc, hc)])
+        else:
+            load(src, wa.at[i])
+
+    load_columns(w_ck, 4)
+    load_columns(w_cv, 5)
 
     barrier = pltpu.get_barrier_semaphore()
 
@@ -135,7 +134,7 @@
     wide = tokens[0].astype(F32)
     nbuf[z] = (wide * lax.rsqrt(jnp.mean(wide * wide, axis=-1, keepdims=True) + 1e-06)).astype(BF16)
     pl.semaphore_wait(
-        barrier, n_chip + jnp.where(has_left, 1, 0) + jnp.where(has_right, 1, 0)
+        barrier, len(peers) + 1 + jnp.where(has_left, 1, 0) + jnp.where(has_right, 1, 0)
     )
 
     def n_copy(b, side):
@@ -172,17 +171,23 @@
     def project_kv(b):
         x = nbuf[b]
         index = v * n_strip + b
-        kv[index, :, 0:hc] = dot(x, wa[4]).astype(BF16)
-        kv[index, :, hc : 2 * hc] = dot(x, wa[5]).astype(BF16)
+        if pair == 2:
+            kv[index] = dot(x, wa[2]).astype(BF16)
+        else:
+            kv[index, :, 0:hc] = dot(x, wa[4]).astype(BF16)
+            kv[index, :, hc : 2 * hc] = dot(x, wa[5]).astype(BF16)
         share(b)
 
-    def project_rest(b):
+    def project_qkv(b):
         def one(i, carry):
-            proj[i, b] = dot(nbuf[b], wa[i]).astype(BF16)
+            product = dot(nbuf[b], wa[i]).astype(BF16)
+            for half in range(pair):
+                proj[pair * i + half, b] = product[:, half * hc : (half + 1) * hc]
             return carry
 
-        lax.fori_loop(0, 4, one, 0)
-
+        lax.fori_loop(0, 4 // pair, one, 0)
+
+    def project_mlp(b):
         def mlp(j, carry):
             hidden = jax.nn.gelu(dot(nbuf[b], wm[j])).astype(BF16)
             term = dot(hidden, md[j])
@@ -204,7 +209,7 @@
         def _():
             fn(z - d)
 
-        @pl.when(z + d < n_strip)
+        @pl.when(jnp.logical_and(z + d < n_strip, d > 0))
         def _():
             fn(z + d)
 
@@ -215,13 +220,26 @@
     @pl.when(has_right)
     def _():
         n_copy(z, 1).start()
+
+    load_columns(w_sq, 0)
+    load_columns(w_sk, 1)
+    load_columns(w_sv, 2)
+    load_columns(w_cq, 3)
+    for j in range(n_up):
+        load(w_up.at[:, pl.ds(j * up, up)], wm.at[j])
+    for j in range(n_up):
+        load(w_down.at[pl.ds(j * up, up)], md.at[j])
+    load(w_so, wo.at[pl.ds(0, hc)])
+    load(w_co, wo.at[pl.ds(hc, hc)])
+    load(ids_in, ids)
+    load(counts_in, counts)
 
     for copy in loads[:2]:
         copy.wait()
     project_kv(z)
     for copy in loads[2:]:
         copy.wait()
-    project_rest(z)
+    project_qkv(z)
 
     def gather_step(d, carry):
         @pl.when(z - d >= 0)
@@ -253,32 +271,49 @@
             lax.fori_loop(0, 2, one, 0)
 
         both(project_kv)
-        both(project_rest)
-
-        @pl.when(d == 1)
-        def _():
-            forward(z)
-
-        @pl.when(d > 1)
-        def _():
-            both_prev = d - 1
-            at_distance(both_prev, forward)
-
+        both(project_qkv)
+
+        def mlp_at(before, c):
+            e = d - before
+
+            @pl.when(jnp.logical_and(before == 0, z - d >= 0))
+            def _():
+                project_mlp(z - d)
+
+            right_now = jnp.logical_and(before == 0, z - d < 0)
+            right_late = jnp.logical_and(before == 1, z - e >= 0)
+            due = jnp.logical_and(jnp.logical_or(right_now, right_late), e > 0)
+
+            @pl.when(jnp.logical_and(due, z + e < n_strip))
+            def _():
+                project_mlp(z + e)
+
+            return c
+
+        lax.fori_loop(0, 2, mlp_at, 0)
+        at_distance(d - 1, forward)
         return carry
 
     lax.fori_loop(1, n_strip, gather_step, 0)
 
-    def self_strip(s, carry):
+    def nth(i):
+        low = n_strip - 1 - i
+        low = jnp.where(low > z, low, low - 1)
+        high = jnp.where(i < z, i, i + 1)
+        return jnp.where(i == n_strip - 1, z, jnp.where(z < n_strip // 2, low, high))
+
+    def self_strip(i, carry):
+        s = nth(i)
+
         def columns(i):
             return lambda lo, hi: proj[i, :, :, lo:hi].reshape(n_strip * rows, hi - lo)
 
-        mixed = attend(proj[0, s], columns(1), columns(2), None)
-        acc[s] = acc[s] + dot(mixed, wo[0])
+        proj[0, s] = attend(proj[0, s], columns(1), columns(2), None)
         return carry
 
-    lax.fori_loop(0, n_strip, self_strip, 0)
-
+    lax.fori_loop(0, n_strip - 2, self_strip, 0)
     at_distance(n_strip - 1, forward)
+    lax.fori_loop(n_strip - 2, n_strip - 1, self_strip, 0)
 
     def from_mate(t, carry):
         kv_copy(mate, t, mate, fwd_send.at[0, t]).wait_recv()
@@ -309,18 +344,11 @@
             device_id_type=MESH,
         ).wait_recv()
 
-    def nth(i):
-        low = n_strip - 1 - i
-        low = jnp.where(low > z, low, low - 1)
-        high = jnp.where(i < z, i, i + 1)
-        return jnp.where(i == n_strip - 1, z, jnp.where(z < n_strip // 2, low, high))
-
     def cross_strip(i, carry):
         s = nth(i)
-        base = (v * n_strip + s) * slots
         for k in range(slots):
-            kbuf[k] = kv[ids[base + k]]
-        count = counts[v * n_strip + s]
+            kbuf[k] = kv[ids[k, s, v]]
+        count = counts[s, v]
         column = lax.broadcasted_iota(jnp.int32, (1, slots * rows), 1)
         bias = jnp.where(column < count * rows, 0.0, -1e30).astype(F32)
 
@@ -328,7 +356,7 @@
             return lambda lo, hi: kbuf[:, :, start + lo : start + hi].reshape(slots * rows, hi - lo)
 
         mixed = attend(proj[3, s], columns(0), columns(hc), bias)
-        acc[s] = acc[s] + dot(mixed, wo[1])
+        acc[s] = acc[s] + dot(jnp.concatenate([proj[0, s], mixed], axis=1), wo[...])
 
         @pl.when(jnp.logical_and(s > z, z == 0))
         def _():
@@ -342,7 +370,6 @@
 
         return carry
 
-    lax.fori_loop(0, n_strip, cross_strip, 0)
 
     def pass_on(i, carry):
         s = nth(i)
@@ -361,7 +388,15 @@
 
         return carry
 
-    lax.fori_loop(0, n_strip - 1, pass_on, 0)
+    lax.fori_loop(0, n_strip - 1, cross_strip, 0)
+
+    last = n_strip - 1
+    self_strip(last, 0)
+    lax.fori_loop(0, min(1, last), pass_on, 0)
+    project_mlp(z)
+    lax.fori_loop(1, min(2, last), pass_on, 0)
+    cross_strip(last, 0)
+    lax.fori_loop(2, max(2, last), pass_on, 0)
 
     @pl.when(has_left)
     def _():
@@ -407,21 +442,23 @@
     hc = weights[0].shape[1]
     hidden = weights[-2].shape[1]
     slots = source_ids.shape[2]
-    up = next(u for u in (384, 256, 128, hidden) if hidden % u == 0)
+    up = next(u for u in (768, 512, 256, 128, hidden) if hidden % u == 0)
     n_up = hidden // up
+    pair = 2 if hc % LANES == 0 else 1
     n_chip = n_view // 2
     dma = pltpu.SemaphoreType.DMA
-    smem = pl.BlockSpec(memory_space=pltpu.SMEM)
     vmem = pl.BlockSpec(memory_space=pltpu.VMEM)
     hbm = pl.BlockSpec(memory_space=pl.ANY)
     return pl.pallas_call(
         functools.partial(kernel, n_view, n_strip, slots),
         out_shape=jax.ShapeDtypeStruct(tokens.shape, tokens.dtype),
-        in_specs=[smem, smem, vmem] + [hbm] * len(weights),
+        in_specs=[hbm, hbm, vmem] + [hbm] * len(weights),
         out_specs=vmem,
         scratch_shapes=[
-            pltpu.VMEM((6, width, hc), BF16),
-            pltpu.VMEM((2, hc, width), BF16),
+            pltpu.SMEM(source_ids.shape[::-1], jnp.int32),
+            pltpu.SMEM(source_count.shape[::-1], jnp.int32),
+            pltpu.VMEM((6 // pair, width, pair * hc), BF16),
+            pltpu.VMEM((2 * hc, width), BF16),
             pltpu.VMEM((n_up, width, up), BF16),
             pltpu.VMEM((n_up, up, width), BF16),
             pltpu.VMEM((n_strip, rows, width), BF16),
@@ -431,7 +468,7 @@
             pltpu.VMEM((n_strip, rows, width), F32),
             pltpu.VMEM((n_strip, rows, width), BF16),
             pltpu.VMEM((n_strip + 1, rows, width), BF16),
-            dma((8 + 2 * n_up,)),
+            dma((10 + 2 * n_up,)),
             dma((2, n_strip)),
             dma((n_strip,)),
             dma((n_chip, n_strip)),
@@ -443,7 +480,7 @@
         compiler_params=pltpu.CompilerParams(
             collective_id=0, has_side_effects=True, vmem_limit_bytes=60 * 1024 * 1024
         ),
-    )(source_ids.reshape(-1), source_count.reshape(-1), tokens, *weights)
+    )(source_ids.transpose(2, 1, 0), source_count.T, tokens, *weights)
 
 
 def solution(mesh):

time: 88.2 us -> 81.8 us (0.927)
  local copies, waits for them, and re-layouts: 4.65 us -> 1.77 us
  Pallas kernels: 82.5 us -> 79.8 us
    pallas_call x1, Pallas kernels: 82.5 us -> 79.8 us  [per_device(): pl.pallas_call(functools.partial(kernel, n_view, n_strip, slots), out_sha...]
    unnamed x3 -> x1, local copies, waits for them, and re-layouts: 3.32 us -> 1.77 us
    reshape x2 -> x0, local copies, waits for them, and re-layouts: 1.33 us -> none  [the longest x1 0.68 us: per_device(): source_ids.reshape(-1)]
where the time goes in v3:
time: 81.8 us; the launch traced here: 81.6 us
  Pallas kernels  79.8 us (98%)
  local copies, waits for them, and re-layouts  1.77 us (2%)
    pallas_call x1, Pallas kernels, per_device(): pl.pallas_call(functools.partial(kernel, n_view, n_strip, slots), out_sha...  79.8 us
    unnamed x1, local copies, waits for them, and re-layouts  1.77 us

profile of v3, /device:TPU:0, one launch (start us, length us, event | category | flops | bytes accessed | tf_op | source)
XLA Modules:
  0.0 81.6 jit_solution(5146497796483137320)
XLA Ops:
  0.0 79.8 %shard_map.127 = bf16[1,128,1536]{2,1,0:T(8,128)(2,1)} custom-call(s32[5,4,8]{2,1,0:T(4,128)} %bitcast.2, s32[4,8]{1,0:T(4,128)} %bitcast.3, bf16[1,128,1536]{2,1,0:T(8,128)(2,1)} %tokens.1, bf16[1536,384]{1,0:T(8,128)(2,1)} %w_sq.1, bf16[1536,384]{1,0:T(8,128)(2,1)} %w_sk.1, bf16[1536,384]{1,0:T(8,128)(2,1)} %w_sv.1, bf16[384,1536]{1,0:T(8,128)(2,1)} %w_so.1, ...), custom_call_target="tpu_custom_call" | custom-call | tf_op jit(solution)/shard_map/pallas_call | solution.py:452
  79.8 1.8 %copy.15 = bf16[1,128,1536]{2,1,0:T(8,128)(2,1)} copy(bf16[1,128,1536]{2,1,0:T(8,128)(2,1)} %shard_map.127) | data formatting | bytes 786432

commit v4 on v3

--- a/solution.py
+++ b/solution.py
@@ -31,17 +31,22 @@
         q_block = q[:, lo:hi] * jnp.asarray(1.0 / math.sqrt(HEAD_DIM), BF16)
         k_block, v_block = keys(lo, hi), values(lo, hi)
         lane = lax.broadcasted_iota(jnp.int32, q_block.shape, 1)
-        result = None
-        for head in range((hi - lo) // HEAD_DIM):
-            inside = jnp.logical_and(lane >= head * HEAD_DIM, lane < (head + 1) * HEAD_DIM)
-            scores = dot_nt(jnp.where(inside, q_block, jnp.zeros_like(q_block)), k_block)
-            if bias is not None:
-                scores = scores + bias
-            top = jnp.max(scores, axis=-1, keepdims=True)
-            weights = jnp.exp(scores - top)
-            total = jnp.sum(weights, axis=-1, keepdims=True)
-            mixed = dot(weights.astype(BF16), v_block) * (1.0 / total)
-            result = mixed if result is None else jnp.where(inside, mixed, result)
+        heads = (hi - lo) // HEAD_DIM
+        inside = [
+            jnp.logical_and(lane >= h * HEAD_DIM, lane < (h + 1) * HEAD_DIM) for h in range(heads)
+        ]
+        stacked = jnp.concatenate([jnp.where(m, q_block, jnp.zeros_like(q_block)) for m in inside])
+        scores = dot_nt(stacked, k_block)
+        if bias is not None:
+            scores = scores + bias
+        top = jnp.max(scores, axis=-1, keepdims=True)
+        weights = jnp.exp(scores - top)
+        total = jnp.sum(weights, axis=-1, keepdims=True)
+        mixed = dot(weights.astype(BF16), v_block) * (1.0 / total)
+        count = q.shape[0]
+        result = mixed[:count]
+        for h in range(1, heads):
+            result = jnp.where(inside[h], mixed[h * count : (h + 1) * count], result)
         parts.append(result.astype(BF16))
     return parts[0] if len(parts) == 1 else jnp.concatenate(parts, axis=1)
 
@@ -311,9 +316,16 @@
         proj[0, s] = attend(proj[0, s], columns(1), columns(2), None)
         return carry
 
-    lax.fori_loop(0, n_strip - 2, self_strip, 0)
-    at_distance(n_strip - 1, forward)
-    lax.fori_loop(n_strip - 2, n_strip - 1, self_strip, 0)
+    def self_first(i, carry):
+        self_strip(i, 0)
+
+        @pl.when(i == 0)
+        def _():
+            at_distance(n_strip - 1, forward)
+
+        return carry
+
+    lax.fori_loop(0, 2, self_first, 0)
 
     def from_mate(t, carry):
         kv_copy(mate, t, mate, fwd_send.at[0, t]).wait_recv()
@@ -388,15 +400,25 @@
 
         return carry
 
-    lax.fori_loop(0, n_strip - 1, cross_strip, 0)
-
     last = n_strip - 1
-    self_strip(last, 0)
-    lax.fori_loop(0, min(1, last), pass_on, 0)
-    project_mlp(z)
-    lax.fori_loop(1, min(2, last), pass_on, 0)
-    cross_strip(last, 0)
-    lax.fori_loop(2, max(2, last), pass_on, 0)
+
+    def sum_step(i, carry):
+        @pl.when(i == last)
+        def _():
+            pass_on(0, 0)
+            project_mlp(z)
+            lax.fori_loop(1, min(2, last), pass_on, 0)
+
+        cross_strip(i, 0)
+
+        @pl.when(i + 2 < n_strip)
+        def _():
+            self_strip(i + 2, 0)
+
+        return carry
+
+    lax.fori_loop(0, n_strip, sum_step, 0)
+    lax.fori_loop(min(2, last), last, pass_on, 0)
 
     @pl.when(has_left)
     def _():

time: 81.8 us -> 81 us (level)
  no operation moved by 1% of the time
where the time goes in v4:
time: 81 us; the launch traced here: 80.8 us
  Pallas kernels  79 us (98%)
  local copies, waits for them, and re-layouts  1.77 us (2%)
    pallas_call x1, Pallas kernels, per_device(): pl.pallas_call(functools.partial(kernel, n_view, n_strip, slots), out_sha...  79 us
    unnamed x1, local copies, waits for them, and re-layouts  1.77 us

profile of v4, /device:TPU:0, one launch (start us, length us, event | category | flops | bytes accessed | tf_op | source)
XLA Modules:
  0.0 80.8 jit_solution(480657759537937416)
XLA Ops:
  0.0 79.0 %shard_map.127 = bf16[1,128,1536]{2,1,0:T(8,128)(2,1)} custom-call(s32[5,4,8]{2,1,0:T(4,128)} %bitcast.2, s32[4,8]{1,0:T(4,128)} %bitcast.3, bf16[1,128,1536]{2,1,0:T(8,128)(2,1)} %tokens.1, bf16[1536,384]{1,0:T(8,128)(2,1)} %w_sq.1, bf16[1536,384]{1,0:T(8,128)(2,1)} %w_sk.1, bf16[1536,384]{1,0:T(8,128)(2,1)} %w_sv.1, bf16[384,1536]{1,0:T(8,128)(2,1)} %w_so.1, ...), custom_call_target="tpu_custom_call" | custom-call | tf_op jit(solution)/shard_map/pallas_call | solution.py:474
  79.0 1.8 %copy.15 = bf16[1,128,1536]{2,1,0:T(8,128)(2,1)} copy(bf16[1,128,1536]{2,1,0:T(8,128)(2,1)} %shard_map.127) | data formatting | bytes 786432

commit v5 on v4

--- a/solution.py
+++ b/solution.py
@@ -10,6 +10,7 @@
 
 HEAD_DIM = 64
 LANES = 128
+PARTS = 2
 MESH = pl.DeviceIdType.MESH
 F32 = jnp.float32
 BF16 = jnp.bfloat16
@@ -98,6 +99,7 @@
     mate = chip * 2 + 1 - core
     rows = tokens.shape[1]
     hc = w_sq.shape[1]
+    part = rows // PARTS
     n_up, _, up = wm.shape
     pair = wa.shape[2] // hc
     has_left, has_right = z > 0, z < n_strip - 1
@@ -142,46 +144,54 @@
         barrier, len(peers) + 1 + jnp.where(has_left, 1, 0) + jnp.where(has_right, 1, 0)
     )
 
-    def n_copy(b, side):
+    def piece(ref, index, h):
+        return ref.at[index, pl.ds(pl.multiple_of(h * part, part), part)]
+
+    def n_copy(b, side, h):
         return pltpu.make_async_remote_copy(
-            src_ref=nbuf.at[b],
-            dst_ref=nbuf.at[b],
-            send_sem=n_send.at[side, b],
-            recv_sem=n_recv.at[b],
+            src_ref=piece(nbuf, b, h),
+            dst_ref=piece(nbuf, b, h),
+            send_sem=n_send.at[side, b, h],
+            recv_sem=n_recv.at[b, h],
             device_id=(v, z + (2 * side - 1)),
             device_id_type=MESH,
         )
 
-    def kv_copy(view, t, to, sem):
+    def kv_copy(view, t, h, to, sem):
         index = view * n_strip + t
         return pltpu.make_async_remote_copy(
-            src_ref=kv.at[index],
-            dst_ref=kv.at[index],
+            src_ref=piece(kv, index, h),
+            dst_ref=piece(kv, index, h),
             send_sem=sem,
-            recv_sem=kv_recv.at[index],
+            recv_sem=kv_recv.at[index, h],
             device_id=(to, z),
             device_id_type=MESH,
         )
 
-    def share(t):
+    def share(t, h):
         for o, p in enumerate(peers):
-            kv_copy(v, t, p, kv_send.at[o, t]).start()
-        kv_copy(v, t, mate, kv_send.at[n_chip - 1, t]).start()
+            kv_copy(v, t, h, p, kv_send.at[o, t, h]).start()
+        kv_copy(v, t, h, mate, kv_send.at[n_chip - 1, t, h]).start()
 
     def forward(t):
-        for o, p in enumerate(peers):
-            kv_copy(p, t, mate, fwd_send.at[o, t]).wait_recv()
-            kv_copy(p, t, mate, fwd_send.at[o, t]).start()
-
-    def project_kv(b):
-        x = nbuf[b]
+        def one(h, carry):
+            for o, p in enumerate(peers):
+                kv_copy(p, t, h, mate, fwd_send.at[o, t, h]).wait_recv()
+                kv_copy(p, t, h, mate, fwd_send.at[o, t, h]).start()
+            return carry
+
+        lax.fori_loop(0, PARTS, one, 0)
+
+    def project_kv(b, h):
+        here = pl.ds(pl.multiple_of(h * part, part), part)
+        x = nbuf[b, here]
         index = v * n_strip + b
         if pair == 2:
-            kv[index] = dot(x, wa[2]).astype(BF16)
+            kv[index, here] = dot(x, wa[2]).astype(BF16)
         else:
-            kv[index, :, 0:hc] = dot(x, wa[4]).astype(BF16)
-            kv[index, :, hc : 2 * hc] = dot(x, wa[5]).astype(BF16)
-        share(b)
+            kv[index, here, 0:hc] = dot(x, wa[4]).astype(BF16)
+            kv[index, here, hc : 2 * hc] = dot(x, wa[5]).astype(BF16)
+        share(b, h)
 
     def project_qkv(b):
         def one(i, carry):
@@ -218,13 +228,15 @@
         def _():
             fn(z + d)
 
-    @pl.when(has_left)
-    def _():
-        n_copy(z, 0).start()
-
-    @pl.when(has_right)
-    def _():
-        n_copy(z, 1).start()
+    for h in range(PARTS):
+
+        @pl.when(has_left)
+        def _():
+            n_copy(z, 0, h).start()
+
+        @pl.when(has_right)
+        def _():
+            n_copy(z, 1, h).start()
 
     load_columns(w_sq, 0)
     load_columns(w_sk, 1)
@@ -241,30 +253,19 @@
 
     for copy in loads[:2]:
         copy.wait()
-    project_kv(z)
+
+    def own_kv(h, carry):
+        project_kv(z, h)
+        return carry
+
+    lax.fori_loop(0, PARTS, own_kv, 0)
     for copy in loads[2:]:
         copy.wait()
     project_qkv(z)
 
     def gather_step(d, carry):
-        @pl.when(z - d >= 0)
-        def _():
-            n_copy(z - d, 1).wait_recv()
-
-            @pl.when(has_right)
-            def _():
-                n_copy(z - d, 1).start()
-
-        @pl.when(z + d < n_strip)
-        def _():
-            n_copy(z + d, 0).wait_recv()
-
-            @pl.when(has_left)
-            def _():
-                n_copy(z + d, 0).start()
-
-        def both(fn):
-            def one(side, c):
+        def one(fn):
+            def side_step(side, c):
                 b = z + (2 * side - 1) * d
 
                 @pl.when(jnp.logical_and(b >= 0, b < n_strip))
@@ -273,33 +274,43 @@
 
                 return c
 
-            lax.fori_loop(0, 2, one, 0)
-
-        both(project_kv)
-        both(project_qkv)
-
-        def mlp_at(before, c):
-            e = d - before
-
-            @pl.when(jnp.logical_and(before == 0, z - d >= 0))
-            def _():
-                project_mlp(z - d)
-
-            right_now = jnp.logical_and(before == 0, z - d < 0)
-            right_late = jnp.logical_and(before == 1, z - e >= 0)
-            due = jnp.logical_and(jnp.logical_or(right_now, right_late), e > 0)
-
-            @pl.when(jnp.logical_and(due, z + e < n_strip))
-            def _():
-                project_mlp(z + e)
+            lax.fori_loop(0, 2, side_step, 0)
+
+        def arrive(h, c):
+            @pl.when(z - d >= 0)
+            def _():
+                n_copy(z - d, 1, h).wait_recv()
+
+                @pl.when(has_right)
+                def _():
+                    n_copy(z - d, 1, h).start()
+
+            @pl.when(z + d < n_strip)
+            def _():
+                n_copy(z + d, 0, h).wait_recv()
+
+                @pl.when(has_left)
+                def _():
+                    n_copy(z + d, 0, h).start()
+
+            one(lambda b: project_kv(b, h))
+
+            late = z + (2 * h - 1) * (d - 1)
+
+            @pl.when((h < 2) & (d > 1) & (late >= 0) & (late < n_strip))
+            def _():
+                project_mlp(late)
 
             return c
 
-        lax.fori_loop(0, 2, mlp_at, 0)
+        lax.fori_loop(0, PARTS, arrive, 0)
+        one(project_qkv)
         at_distance(d - 1, forward)
         return carry
 
     lax.fori_loop(1, n_strip, gather_step, 0)
+    at_distance(n_strip - 1, project_mlp)
+    at_distance(n_strip - 1, forward)
 
     def nth(i):
         low = n_strip - 1 - i
@@ -316,45 +327,40 @@
         proj[0, s] = attend(proj[0, s], columns(1), columns(2), None)
         return carry
 
-    def self_first(i, carry):
-        self_strip(i, 0)
-
-        @pl.when(i == 0)
-        def _():
-            at_distance(n_strip - 1, forward)
-
-        return carry
-
-    lax.fori_loop(0, 2, self_first, 0)
+    self_strip(0, 0)
 
     def from_mate(t, carry):
-        kv_copy(mate, t, mate, fwd_send.at[0, t]).wait_recv()
-        for p in peers:
-            kv_copy(p + 1 - 2 * core, t, mate, fwd_send.at[0, t]).wait_recv()
+        def one(h, c):
+            kv_copy(mate, t, h, mate, fwd_send.at[0, t, h]).wait_recv()
+            for p in peers:
+                kv_copy(p + 1 - 2 * core, t, h, mate, fwd_send.at[0, t, h]).wait_recv()
+            return c
+
+        lax.fori_loop(0, PARTS, one, 0)
         return carry
 
     lax.fori_loop(0, n_strip, from_mate, 0)
 
-    def rs_copy(s, side):
-        slot = jnp.where(jnp.logical_and(side == 0, s == z - 1), n_strip, s)
+    def rs_copy(s, side, h, slot=None):
+        if slot is None:
+            slot = jnp.where(jnp.logical_and(side == 0, s == z - 1), n_strip, s)
         return pltpu.make_async_remote_copy(
-            src_ref=rs_send.at[s],
-            dst_ref=rs_recv.at[slot],
-            send_sem=rs_ssem.at[s],
-            recv_sem=rs_rsem.at[slot],
+            src_ref=piece(rs_send, s, h),
+            dst_ref=piece(rs_recv, slot, h),
+            send_sem=rs_ssem.at[s, h],
+            recv_sem=rs_rsem.at[slot, h],
             device_id=(v, z + (2 * side - 1)),
             device_id_type=MESH,
         )
 
-    def rs_wait(slot, side):
-        pltpu.make_async_remote_copy(
-            src_ref=rs_send.at[0],
-            dst_ref=rs_recv.at[slot],
-            send_sem=rs_ssem.at[0],
-            recv_sem=rs_rsem.at[slot],
-            device_id=(v, z + (2 * side - 1)),
-            device_id_type=MESH,
-        ).wait_recv()
+    def send_sum(s, side, h, arrived):
+        here = pl.ds(pl.multiple_of(h * part, part), part)
+        total = acc[s, here]
+        if arrived:
+            rs_copy(0, side, h, s).wait_recv()
+            total = total + rs_recv[s, here].astype(F32)
+        rs_send[s, here] = total.astype(BF16)
+        rs_copy(s, side, h).start()
 
     def cross_strip(i, carry):
         s = nth(i)
@@ -370,34 +376,35 @@
         mixed = attend(proj[3, s], columns(0), columns(hc), bias)
         acc[s] = acc[s] + dot(jnp.concatenate([proj[0, s], mixed], axis=1), wo[...])
 
-        @pl.when(jnp.logical_and(s > z, z == 0))
-        def _():
-            rs_send[s] = acc[s].astype(BF16)
-            rs_copy(s, 1).start()
-
-        @pl.when(jnp.logical_and(s < z, z == n_strip - 1))
-        def _():
-            rs_send[s] = acc[s].astype(BF16)
-            rs_copy(s, 0).start()
-
-        return carry
-
+        def start(h, c):
+            @pl.when(jnp.logical_and(s > z, z == 0))
+            def _():
+                send_sum(s, 1, h, False)
+
+            @pl.when(jnp.logical_and(s < z, z == n_strip - 1))
+            def _():
+                send_sum(s, 0, h, False)
+
+            return c
+
+        lax.fori_loop(0, PARTS, start, 0)
+        return carry
 
     def pass_on(i, carry):
         s = nth(i)
 
-        @pl.when(jnp.logical_and(s > z, has_left))
-        def _():
-            rs_wait(s, 1)
-            rs_send[s] = (acc[s] + rs_recv[s].astype(F32)).astype(BF16)
-            rs_copy(s, 1).start()
-
-        @pl.when(jnp.logical_and(s < z, has_right))
-        def _():
-            rs_wait(s, 0)
-            rs_send[s] = (acc[s] + rs_recv[s].astype(F32)).astype(BF16)
-            rs_copy(s, 0).start()
-
+        def one(h, c):
+            @pl.when(jnp.logical_and(s > z, has_left))
+            def _():
+                send_sum(s, 1, h, True)
+
+            @pl.when(jnp.logical_and(s < z, has_right))
+            def _():
+                send_sum(s, 0, h, True)
+
+            return c
+
+        lax.fori_loop(0, PARTS, one, 0)
         return carry
 
     last = n_strip - 1
@@ -411,49 +418,59 @@
 
         cross_strip(i, 0)
 
-        @pl.when(i + 2 < n_strip)
-        def _():
-            self_strip(i + 2, 0)
+        @pl.when(i + 1 < n_strip)
+        def _():
+            self_strip(i + 1, 0)
 
         return carry
 
     lax.fori_loop(0, n_strip, sum_step, 0)
     lax.fori_loop(min(2, last), last, pass_on, 0)
 
-    @pl.when(has_left)
-    def _():
-        rs_wait(z, 1)
-        acc[z] = acc[z] + rs_recv[z].astype(F32)
-
-    @pl.when(has_right)
-    def _():
-        rs_wait(n_strip, 0)
-        acc[z] = acc[z] + rs_recv[n_strip].astype(F32)
-
-    out[0] = (tokens[0].astype(F32) + acc[z]).astype(BF16)
+    def finish(h, carry):
+        here = pl.ds(pl.multiple_of(h * part, part), part)
+
+        @pl.when(has_left)
+        def _():
+            rs_copy(0, 1, h, z).wait_recv()
+            acc[z, here] = acc[z, here] + rs_recv[z, here].astype(F32)
+
+        @pl.when(has_right)
+        def _():
+            rs_copy(0, 0, h, n_strip).wait_recv()
+            acc[z, here] = acc[z, here] + rs_recv[n_strip, here].astype(F32)
+
+        out[0, here] = (tokens[0, here].astype(F32) + acc[z, here]).astype(BF16)
+        return carry
+
+    lax.fori_loop(0, PARTS, finish, 0)
 
     def settle(t, carry):
-        @pl.when(jnp.logical_and(has_left, t >= z))
-        def _():
-            n_copy(t, 0).wait_send()
-
-        @pl.when(jnp.logical_and(has_right, t <= z))
-        def _():
-            n_copy(t, 1).wait_send()
-
-        for o, p in enumerate(peers):
-            kv_copy(v, t, p, kv_send.at[o, t]).wait_send()
-            kv_copy(p, t, mate, fwd_send.at[o, t]).wait_send()
-        kv_copy(v, t, mate, kv_send.at[n_chip - 1, t]).wait_send()
-
-        @pl.when(t > z)
-        def _():
-            rs_copy(t, 1).wait_send()
-
-        @pl.when(t < z)
-        def _():
-            rs_copy(t, 0).wait_send()
-
+        def one(h, c):
+            @pl.when(jnp.logical_and(has_left, t >= z))
+            def _():
+                n_copy(t, 0, h).wait_send()
+
+            @pl.when(jnp.logical_and(has_right, t <= z))
+            def _():
+                n_copy(t, 1, h).wait_send()
+
+            for o, p in enumerate(peers):
+                kv_copy(v, t, h, p, kv_send.at[o, t, h]).wait_send()
+                kv_copy(p, t, h, mate, fwd_send.at[o, t, h]).wait_send()
+            kv_copy(v, t, h, mate, kv_send.at[n_chip - 1, t, h]).wait_send()
+
+            @pl.when(t > z)
+            def _():
+                rs_copy(t, 1, h).wait_send()
+
+            @pl.when(t < z)
+            def _():
+                rs_copy(t, 0, h).wait_send()
+
+            return c
+
+        lax.fori_loop(0, PARTS, one, 0)
         return carry
 
     lax.fori_loop(0, n_strip, settle, 0)
@@ -491,13 +508,13 @@
             pltpu.VMEM((n_strip, rows, width), BF16),
             pltpu.VMEM((n_strip + 1, rows, width), BF16),
             dma((10 + 2 * n_up,)),
-            dma((2, n_strip)),
-            dma((n_strip,)),
-            dma((n_chip, n_strip)),
-            dma((n_chip, n_strip)),
-            dma((n_view * n_strip,)),
-            dma((n_strip,)),
-            dma((n_strip + 1,)),
+            dma((2, n_strip, PARTS)),
+            dma((n_strip, PARTS)),
+            dma((n_chip, n_strip, PARTS)),
+            dma((n_chip, n_strip, PARTS)),
+            dma((n_view * n_strip, PARTS)),
+            dma((n_strip, PARTS)),
+            dma((n_strip + 1, PARTS)),
         ],
         compiler_params=pltpu.CompilerParams(
             collective_id=0, has_side_effects=True, vmem_limit_bytes=60 * 1024 * 1024

time: 81 us -> 79.2 us (0.978)
  Pallas kernels: 79 us -> 77.2 us
    pallas_call x1, Pallas kernels: 79 us -> 77.2 us  [per_device(): pl.pallas_call(functools.partial(kernel, n_view, n_strip, slots), out_sha...]
where the time goes in v5:
time: 79.2 us; the launch traced here: 79 us
  Pallas kernels  77.2 us (97%)
  local copies, waits for them, and re-layouts  1.77 us (2%)
    pallas_call x1, Pallas kernels, per_device(): pl.pallas_call(functools.partial(kernel, n_view, n_strip, slots), out_sha...  77.2 us
    unnamed x1, local copies, waits for them, and re-layouts  1.77 us

profile of v5, /device:TPU:0, one launch (start us, length us, event | category | flops | bytes accessed | tf_op | source)
XLA Modules:
  0.0 79.0 jit_solution(12208335438802342562)
XLA Ops:
  0.0 77.2 %shard_map.127 = bf16[1,128,1536]{2,1,0:T(8,128)(2,1)} custom-call(s32[5,4,8]{2,1,0:T(4,128)} %bitcast.2, s32[4,8]{1,0:T(4,128)} %bitcast.3, bf16[1,128,1536]{2,1,0:T(8,128)(2,1)} %tokens.1, bf16[1536,384]{1,0:T(8,128)(2,1)} %w_sq.1, bf16[1536,384]{1,0:T(8,128)(2,1)} %w_sk.1, bf16[1536,384]{1,0:T(8,128)(2,1)} %w_sv.1, bf16[384,1536]{1,0:T(8,128)(2,1)} %w_so.1, ...), custom_call_target="tpu_custom_call" | custom-call | tf_op jit(solution)/shard_map/pallas_call | solution.py:491
  77.2 1.8 %copy.15 = bf16[1,128,1536]{2,1,0:T(8,128)(2,1)} copy(bf16[1,128,1536]{2,1,0:T(8,128)(2,1)} %shard_map.127) | data formatting | bytes 786432

commit v6 on v5

--- a/solution.py
+++ b/solution.py
@@ -11,6 +11,7 @@
 HEAD_DIM = 64
 LANES = 128
 PARTS = 2
+SUM_PARTS = 4
 MESH = pl.DeviceIdType.MESH
 F32 = jnp.float32
 BF16 = jnp.bfloat16
@@ -100,6 +101,7 @@
     rows = tokens.shape[1]
     hc = w_sq.shape[1]
     part = rows // PARTS
+    sum_part = rows // SUM_PARTS
     n_up, _, up = wm.shape
     pair = wa.shape[2] // hc
     has_left, has_right = z > 0, z < n_strip - 1
@@ -144,8 +146,8 @@
         barrier, len(peers) + 1 + jnp.where(has_left, 1, 0) + jnp.where(has_right, 1, 0)
     )
 
-    def piece(ref, index, h):
-        return ref.at[index, pl.ds(pl.multiple_of(h * part, part), part)]
+    def piece(ref, index, h, size=part):
+        return ref.at[index, pl.ds(pl.multiple_of(h * size, size), size)]
 
     def n_copy(b, side, h):
         return pltpu.make_async_remote_copy(
@@ -309,10 +311,10 @@
         return carry
 
     lax.fori_loop(1, n_strip, gather_step, 0)
-    at_distance(n_strip - 1, project_mlp)
-    at_distance(n_strip - 1, forward)
 
     def nth(i):
+        if n_strip > 2:
+            i = jnp.where(i < 2, 1 - i, i)
         low = n_strip - 1 - i
         low = jnp.where(low > z, low, low - 1)
         high = jnp.where(i < z, i, i + 1)
@@ -327,7 +329,16 @@
         proj[0, s] = attend(proj[0, s], columns(1), columns(2), None)
         return carry
 
-    self_strip(0, 0)
+    def self_first(i, carry):
+        self_strip(i, 0)
+
+        @pl.when(i == 0)
+        def _():
+            at_distance(n_strip - 1, forward)
+
+        return carry
+
+    lax.fori_loop(0, 2, self_first, 0)
 
     def from_mate(t, carry):
         def one(h, c):
@@ -345,8 +356,8 @@
         if slot is None:
             slot = jnp.where(jnp.logical_and(side == 0, s == z - 1), n_strip, s)
         return pltpu.make_async_remote_copy(
-            src_ref=piece(rs_send, s, h),
-            dst_ref=piece(rs_recv, slot, h),
+            src_ref=piece(rs_send, s, h, sum_part),
+            dst_ref=piece(rs_recv, slot, h, sum_part),
             send_sem=rs_ssem.at[s, h],
             recv_sem=rs_rsem.at[slot, h],
             device_id=(v, z + (2 * side - 1)),
@@ -354,7 +365,7 @@
         )
 
     def send_sum(s, side, h, arrived):
-        here = pl.ds(pl.multiple_of(h * part, part), part)
+        here = pl.ds(pl.multiple_of(h * sum_part, sum_part), sum_part)
         total = acc[s, here]
         if arrived:
             rs_copy(0, side, h, s).wait_recv()
@@ -387,7 +398,7 @@
 
             return c
 
-        lax.fori_loop(0, PARTS, start, 0)
+        lax.fori_loop(0, SUM_PARTS, start, 0)
         return carry
 
     def pass_on(i, carry):
@@ -404,7 +415,7 @@
 
             return c
 
-        lax.fori_loop(0, PARTS, one, 0)
+        lax.fori_loop(0, SUM_PARTS, one, 0)
         return carry
 
     last = n_strip - 1
@@ -418,9 +429,13 @@
 
         cross_strip(i, 0)
 
-        @pl.when(i + 1 < n_strip)
-        def _():
-            self_strip(i + 1, 0)
+        @pl.when(i == 0)
+        def _():
+            at_distance(n_strip - 1, project_mlp)
+
+        @pl.when(i + 2 < n_strip)
+        def _():
+            self_strip(i + 2, 0)
 
         return carry
 
@@ -428,7 +443,7 @@
     lax.fori_loop(min(2, last), last, pass_on, 0)
 
     def finish(h, carry):
-        here = pl.ds(pl.multiple_of(h * part, part), part)
+        here = pl.ds(pl.multiple_of(h * sum_part, sum_part), sum_part)
 
         @pl.when(has_left)
         def _():
@@ -443,7 +458,7 @@
         out[0, here] = (tokens[0, here].astype(F32) + acc[z, here]).astype(BF16)
         return carry
 
-    lax.fori_loop(0, PARTS, finish, 0)
+    lax.fori_loop(0, SUM_PARTS, finish, 0)
 
     def settle(t, carry):
         def one(h, c):
@@ -460,6 +475,9 @@
                 kv_copy(p, t, h, mate, fwd_send.at[o, t, h]).wait_send()
             kv_copy(v, t, h, mate, kv_send.at[n_chip - 1, t, h]).wait_send()
 
+            return c
+
+        def one_sum(h, c):
             @pl.when(t > z)
             def _():
                 rs_copy(t, 1, h).wait_send()
@@ -471,6 +489,7 @@
             return c
 
         lax.fori_loop(0, PARTS, one, 0)
+        lax.fori_loop(0, SUM_PARTS, one_sum, 0)
         return carry
 
     lax.fori_loop(0, n_strip, settle, 0)
@@ -513,8 +532,8 @@
             dma((n_chip, n_strip, PARTS)),
             dma((n_chip, n_strip, PARTS)),
             dma((n_view * n_strip, PARTS)),
-            dma((n_strip, PARTS)),
-            dma((n_strip + 1, PARTS)),
+            dma((n_strip, SUM_PARTS)),
+            dma((n_strip + 1, SUM_PARTS)),
         ],
         compiler_params=pltpu.CompilerParams(
             collective_id=0, has_side_effects=True, vmem_limit_bytes=60 * 1024 * 1024

time: 79.2 us -> 79.4 us (level)
  no operation moved by 1% of the time
where the time goes in v6:
time: 79.4 us; the launch traced here: 79.2 us
  Pallas kernels  77.4 us (97%)
  local copies, waits for them, and re-layouts  1.77 us (2%)
    pallas_call x1, Pallas kernels, per_device(): pl.pallas_call(functools.partial(kernel, n_view, n_strip, slots), out_sha...  77.4 us
    unnamed x1, local copies, waits for them, and re-layouts  1.77 us

profile of v6, /device:TPU:0, one launch (start us, length us, event | category | flops | bytes accessed | tf_op | source)
XLA Modules:
  0.0 79.2 jit_solution(11127804239133887283)
XLA Ops:
  0.0 77.4 %shard_map.127 = bf16[1,128,1536]{2,1,0:T(8,128)(2,1)} custom-call(s32[5,4,8]{2,1,0:T(4,128)} %bitcast.2, s32[4,8]{1,0:T(4,128)} %bitcast.3, bf16[1,128,1536]{2,1,0:T(8,128)(2,1)} %tokens.1, bf16[1536,384]{1,0:T(8,128)(2,1)} %w_sq.1, bf16[1536,384]{1,0:T(8,128)(2,1)} %w_sk.1, bf16[1536,384]{1,0:T(8,128)(2,1)} %w_sv.1, bf16[384,1536]{1,0:T(8,128)(2,1)} %w_so.1, ...), custom_call_target="tpu_custom_call" | custom-call | tf_op jit(solution)/shard_map/pallas_call | solution.py:510
  77.4 1.8 %copy.15 = bf16[1,128,1536]{2,1,0:T(8,128)(2,1)} copy(bf16[1,128,1536]{2,1,0:T(8,128)(2,1)} %shard_map.127) | data formatting | bytes 786432

commit v7 on v6

--- a/solution.py
+++ b/solution.py
@@ -421,9 +421,12 @@
     last = n_strip - 1
 
     def sum_step(i, carry):
+        @pl.when(i == max(last - 1, 1))
+        def _():
+            pass_on(0, 0)
+
         @pl.when(i == last)
         def _():
-            pass_on(0, 0)
             project_mlp(z)
             lax.fori_loop(1, min(2, last), pass_on, 0)
 

time: 79.4 us -> 79.4 us (level)
  no operation moved by 1% of the time
where the time goes in v7:
time: 79.4 us; the launch traced here: 79.2 us
  Pallas kernels  77.4 us (97%)
  local copies, waits for them, and re-layouts  1.77 us (2%)
    pallas_call x1, Pallas kernels, per_device(): pl.pallas_call(functools.partial(kernel, n_view, n_strip, slots), out_sha...  77.4 us
    unnamed x1, local copies, waits for them, and re-layouts  1.77 us

profile of v7, /device:TPU:0, one launch (start us, length us, event | category | flops | bytes accessed | tf_op | source)
XLA Modules:
  0.0 79.2 jit_solution(9814742491781531088)
XLA Ops:
  0.0 77.4 %shard_map.127 = bf16[1,128,1536]{2,1,0:T(8,128)(2,1)} custom-call(s32[5,4,8]{2,1,0:T(4,128)} %bitcast.2, s32[4,8]{1,0:T(4,128)} %bitcast.3, bf16[1,128,1536]{2,1,0:T(8,128)(2,1)} %tokens.1, bf16[1536,384]{1,0:T(8,128)(2,1)} %w_sq.1, bf16[1536,384]{1,0:T(8,128)(2,1)} %w_sk.1, bf16[1536,384]{1,0:T(8,128)(2,1)} %w_sv.1, bf16[384,1536]{1,0:T(8,128)(2,1)} %w_so.1, ...), custom_call_target="tpu_custom_call" | custom-call | tf_op jit(solution)/shard_map/pallas_call | solution.py:513
  77.4 1.8 %copy.15 = bf16[1,128,1536]{2,1,0:T(8,128)(2,1)} copy(bf16[1,128,1536]{2,1,0:T(8,128)(2,1)} %shard_map.127) | data formatting | bytes 786432
